TPU v7x, 32 devices: a whole 2x2x4 slice. The times are simulated.
32 devices in a mesh: ctx: 8 (over z, core), head: 4 (over y, x).
Axes of the slice: x: 2, y: 2, z: 4, core: 2. Of those that a mesh axis runs over, the one named last changes fastest.
Arguments:
- queries: bfloat16 [2, 12288, 4096], P(None, 'ctx', 'head')
- layer_keys_input: bfloat16 [2, 12288, 2048], P(None, 'ctx', 'head')
- layer_values_input: bfloat16 [2, 12288, 2048], P(None, 'ctx', 'head')
- attn_out: bfloat16 [2, 12288, 4096], P(None, 'ctx', 'head'), as said below
- grad_out: bfloat16 [2, 12288, 4096], P(None, 'ctx', 'head'), may hold values from -6 to 6
- log_norm: float32 [2, 32, 12288], P(None, 'head', 'ctx'), as said below
- window: int32 [2], replicated, may hold values from 512 to 1024, as said below
Outputs:
- grad_query: bfloat16 [2, 12288, 4096], P(None, ('ctx', 'head'))
- grad_key: bfloat16 [2, 12288, 2048], P(None, ('ctx', 'head'))
- grad_value: bfloat16 [2, 12288, 2048], P(None, ('ctx', 'head'))
Inputs may be any that keep to these rules, and one draw needn't show every extreme that they name: Each layer's window is 512 to 1024 tokens; one of the layers has exactly 1024. log_norm is the log of the sum, over each query's window, of exp of its scaled scores against layer_keys_input. attn_out is the attention output that these weights give from layer_values_input.
All inputs are finite; a program needn't handle non-finite values.
Results may differ from a plain program's by a relative error of at most 0.005.
Values may be sent and summed in bfloat16 or wider, within the bound.
No kernel may reach another device: no remote copies, remote signals or barrier semaphores. Data moves between devices by JAX's collectives and lax.ppermute only.
A program may use at most 256 MiB of HBM per device.

v0:
```python
import jax
import jax.numpy as jnp
from jax import lax
from jax.sharding import PartitionSpec as P

HEAD_SIZE = 128
WINDOW_LENGTH = 1024
QUERY_PRE = 168
SLIDING_LAYERS = 2
BLOCK = 512


def shifted(value, axis, steps):
    count = lax.axis_size(axis)
    first, last = (max(0, -steps), min(count, count - steps))
    return lax.ppermute(value, axis, [(source, source + steps) for source in range(first, last)])


def block_grads(q_block, do_block, lse_block, dlt_block, k_block, v_block, q_pos, k_pos, win):
    row_count, head_count, head_dim = q_block.shape
    kv_count = k_block.shape[1]
    query_group_count = head_count // kv_count
    score_scale = QUERY_PRE ** (-0.5)
    query_head_count = q_block.reshape(row_count, kv_count, query_group_count, head_dim)
    do_heads = do_block.reshape(row_count, kv_count, query_group_count, head_dim)
    scores = (
        jnp.einsum("rkgd,ckd->kgrc", query_head_count, k_block, preferred_element_type=jnp.float32)
        * score_scale
    )
    lse_heads = lse_block.reshape(kv_count, query_group_count, row_count)
    dlt_heads = dlt_block.reshape(kv_count, query_group_count, row_count)
    visible = (
        (k_pos[None, :] <= q_pos[:, None])
        & (q_pos[:, None] - k_pos[None, :] < win)
        & (k_pos[None, :] >= 0)
    )
    attn_prob = jnp.where(visible, jnp.exp(scores - lse_heads[..., None]), 0.0)
    prob_low = attn_prob.astype(jnp.bfloat16)
    grad_prob = jnp.einsum("rkgd,ckd->kgrc", do_heads, v_block, preferred_element_type=jnp.float32)
    grad_score = attn_prob * (grad_prob - dlt_heads[..., None])
    score_low = grad_score.astype(jnp.bfloat16)
    dv_part = jnp.einsum("kgrc,rkgd->ckd", prob_low, do_heads, preferred_element_type=jnp.float32)
    dk_part = (
        jnp.einsum(
            "kgrc,rkgd->ckd", score_low, query_head_count, preferred_element_type=jnp.float32
        )
        * score_scale
    )
    dq_part = (
        jnp.einsum("kgrc,ckd->rkgd", score_low, k_block, preferred_element_type=jnp.float32)
        * score_scale
    )
    return (dq_part.reshape(row_count, head_count, head_dim), dk_part, dv_part)


def sweep_blocks(lower, upper, state, layer_parts, offset_tok):
    q_all, do_all, lse_all, dlt_all, k_ext, v_ext, win = layer_parts

    def step(block_idx, carry):
        dq_all, key_gradient_total, value_gradient_total = carry
        start_row = block_idx * BLOCK
        q_block = lax.dynamic_slice_in_dim(q_all, start_row, BLOCK, 0)
        do_block = lax.dynamic_slice_in_dim(do_all, start_row, BLOCK, 0)
        lse_block = lax.dynamic_slice_in_dim(lse_all, start_row, BLOCK, 1)
        dlt_block = lax.dynamic_slice_in_dim(dlt_all, start_row, BLOCK, 1)
        k_block = lax.dynamic_slice_in_dim(k_ext, start_row, WINDOW_LENGTH + BLOCK, 0)
        v_block = lax.dynamic_slice_in_dim(v_ext, start_row, WINDOW_LENGTH + BLOCK, 0)
        q_pos = offset_tok + start_row + jnp.arange(BLOCK, dtype=jnp.int32)
        k_pos = (
            offset_tok
            + start_row
            - WINDOW_LENGTH
            + jnp.arange(WINDOW_LENGTH + BLOCK, dtype=jnp.int32)
        )
        dq_part, dk_part, dv_part = block_grads(
            q_block, do_block, lse_block, dlt_block, k_block, v_block, q_pos, k_pos, win
        )
        dq_all = lax.dynamic_update_slice_in_dim(dq_all, dq_part.astype(jnp.bfloat16), start_row, 0)
        dk_old = lax.dynamic_slice_in_dim(key_gradient_total, start_row, WINDOW_LENGTH + BLOCK, 0)
        dv_old = lax.dynamic_slice_in_dim(value_gradient_total, start_row, WINDOW_LENGTH + BLOCK, 0)
        key_gradient_total = lax.dynamic_update_slice_in_dim(
            key_gradient_total, dk_old + dk_part, start_row, 0
        )
        value_gradient_total = lax.dynamic_update_slice_in_dim(
            value_gradient_total, dv_old + dv_part, start_row, 0
        )
        return (dq_all, key_gradient_total, value_gradient_total)

    if upper <= lower:
        return state
    return lax.fori_loop(lower, upper, step, state)


def send_back(states, tok_local):
    halo_dk = jnp.stack([entry[1][:WINDOW_LENGTH] for entry in states], 0)
    halo_dv = jnp.stack([entry[2][:WINDOW_LENGTH] for entry in states], 0)
    back_dk, back_dv = shifted((halo_dk, halo_dv), "ctx", -1)
    result = []
    for layer_number in range(len(states)):
        dq_all, key_gradient_total, value_gradient_total = states[layer_number]
        key_gradient_total = key_gradient_total.at[tok_local:].add(back_dk[layer_number])
        value_gradient_total = value_gradient_total.at[tok_local:].add(back_dv[layer_number])
        result.append((dq_all, key_gradient_total, value_gradient_total))
    return result


def shards(queries, layer_keys_input, layer_values_input, attn_out, grad_out, log_norm, window):
    tok_local = queries.shape[1]
    head_local = log_norm.shape[1]
    kv_local = layer_keys_input.shape[2] // HEAD_SIZE
    offset_tok = lax.axis_index("ctx") * tok_local
    delta = jnp.sum(
        (grad_out.astype(jnp.float32) * attn_out.astype(jnp.float32)).reshape(
            SLIDING_LAYERS, tok_local, head_local, HEAD_SIZE
        ),
        axis=-1,
    ).transpose(0, 2, 1)
    rim_keys, rim_values = shifted(
        (
            layer_keys_input[:, tok_local - WINDOW_LENGTH :],
            layer_values_input[:, tok_local - WINDOW_LENGTH :],
        ),
        "ctx",
        1,
    )
    all_parts = []
    states = []
    for layer_number in range(SLIDING_LAYERS):
        k_ext = jnp.concatenate(
            [rim_keys[layer_number], layer_keys_input[layer_number]], 0
        ).reshape(WINDOW_LENGTH + tok_local, kv_local, HEAD_SIZE)
        v_ext = jnp.concatenate(
            [rim_values[layer_number], layer_values_input[layer_number]], 0
        ).reshape(WINDOW_LENGTH + tok_local, kv_local, HEAD_SIZE)
        all_parts.append(
            (
                queries[layer_number].reshape(tok_local, head_local, HEAD_SIZE),
                grad_out[layer_number].reshape(tok_local, head_local, HEAD_SIZE),
                log_norm[layer_number],
                delta[layer_number],
                k_ext,
                v_ext,
                window[layer_number],
            )
        )
        states.append(
            (
                jnp.zeros((tok_local, head_local, HEAD_SIZE), jnp.bfloat16),
                jnp.zeros((WINDOW_LENGTH + tok_local, kv_local, HEAD_SIZE), jnp.float32),
                jnp.zeros((WINDOW_LENGTH + tok_local, kv_local, HEAD_SIZE), jnp.float32),
            )
        )
    block_count = tok_local // BLOCK
    for layer_number in range(SLIDING_LAYERS):
        states[layer_number] = sweep_blocks(
            0, block_count, states[layer_number], all_parts[layer_number], offset_tok
        )
    states = send_back(states, tok_local)
    for layer_number in range(SLIDING_LAYERS):
        states[layer_number] = sweep_blocks(
            block_count, block_count, states[layer_number], all_parts[layer_number], offset_tok
        )
    dq_stack = jnp.stack(
        [entry[0].reshape(tok_local, head_local * HEAD_SIZE) for entry in states], 0
    )
    dk_stack = jnp.stack(
        [
            entry[1][WINDOW_LENGTH:].astype(jnp.bfloat16).reshape(tok_local, kv_local * HEAD_SIZE)
            for entry in states
        ],
        0,
    )
    dv_stack = jnp.stack(
        [
            entry[2][WINDOW_LENGTH:].astype(jnp.bfloat16).reshape(tok_local, kv_local * HEAD_SIZE)
            for entry in states
        ],
        0,
    )
    grad_query, grad_key, grad_value = (
        lax.all_to_all(dq_stack, "head", split_axis=1, concat_axis=2, tiled=True),
        lax.all_to_all(dk_stack, "head", split_axis=1, concat_axis=2, tiled=True),
        lax.all_to_all(dv_stack, "head", split_axis=1, concat_axis=2, tiled=True),
    )
    return (grad_query, grad_key, grad_value)


def solution(mesh):
    in_specs = (
        P(None, "ctx", "head"),
        P(None, "ctx", "head"),
        P(None, "ctx", "head"),
        P(None, "ctx", "head"),
        P(None, "ctx", "head"),
        P(None, "head", "ctx"),
        P(),
    )
    out_specs = (
        P(None, ("ctx", "head"), None),
        P(None, ("ctx", "head"), None),
        P(None, ("ctx", "head"), None),
    )
    return jax.shard_map(shards, mesh=mesh, in_specs=in_specs, out_specs=out_specs, check_vma=False)
```

profile of v0, /device:TPU:24, one launch (start us, length us, event | category | flops | bytes accessed | tf_op | source)
XLA Modules:
  0.0 712.4 jit_solution(16135677125912510373)
XLA Ops:
  105.0 198.0 %while.43 = (s32[]{:T(128)}, bf16[1536,8,128]{0,2,1:T(8,128)(2,1)}, f32[2560,4,128]{0,2,1:T(8,128)}, f32[2560,4,128]{0,2,1:T(8,128)}, bf16[2560,4,128]{0,2,1:T(8...) while((s32[]{:T(128)}, bf16[1536,8,128]{0,2,1:T(8,128)(2,1)}, ...), condition=%wide.region_4.5_spmd, body=%wide.region_3.4_spmd.sunk | while | flops 8104449024 | bytes 143838512 | solution.py:91
  108.9 13.0 %fusion.136 = f32[4,2,512,1536]{2,3,1,0:T(8,128)} fusion(bf16[512,4,2,128]{0,3,2,1:T(8,128)(2,1)S(1)} %bitcast.289, f32[4,2,512]{2,1,0:T(2,128)S(1)} %sub.237, pred[512,1536]{0,1:T(8,128)(4,1)S(1)} %fusion.135, bf16[2560,4,128]{0,2,1:T(8,128)(2,1)} %get-tuple-element.1022, s32[]{:T(128)S(6)} %select_n.92), kind=kOutput, calls=%fused_computation.41.clone.1 | convolution fusion | flops 1629487104 | bytes 28590084 | tf_op jit(solution)/shard_map/while/body/eval_jaxpr/rkgd,ckd->kgrc/dot_general | solution.py:27
  121.9 14.9 %fusion.137 = bf16[4,2,512,1536]{2,3,1,0:T(8,128)(2,1)} fusion(f32[4,2,512,1536]{2,3,1,0:T(8,128)} %fusion.136, bf16[512,4,2,128]{0,3,2,1:T(8,128)(2,1)S(1)} %bitcast.281, f32[4,2,512]{2,1,0:T(2,128)S(1)} %sub.239, bf16[2560,4,128]{0,2,1:T(8,128)(2,1)} %get-tuple-element.1027, s32[]{:T(128)S(6)} %select_n.92), kind=kOutput, calls=%fused_computation.38.clone.1 | convolution fusion | flops 1629487104 | bytes 40386564 | tf_op jit(solution)/shard_map/while/body/eval_jaxpr/rkgd,ckd->kgrc/dot_general | solution.py:39
  156.0 15.1 %fusion.138 = f32[2560,4,128]{0,2,1:T(8,128)} fusion(f32[2560,4,128]{0,2,1:T(8,128)} %get-tuple-element.1003, s32[]{:T(128)S(6)} %select_n.92, bf16[512,4,2,128]{0,3,2,1:T(8,128)(2,1)S(1)} %bitcast.282, f32[4,2,512,1536]{2,3,1,0:T(8,128)} %fusion.136), kind=kOutput, calls=%fused_computation.47.clone.1 | convolution fusion | flops 1617690624 | bytes 32505860 | tf_op jit(solution)/shard_map/while/body/eval_jaxpr/kgrc,rkgd->ckd/dot_general | solution.py:42
  174.8 13.0 %fusion.136 = f32[4,2,512,1536]{2,3,1,0:T(8,128)} fusion(bf16[512,4,2,128]{0,3,2,1:T(8,128)(2,1)S(1)} %bitcast.289, f32[4,2,512]{2,1,0:T(2,128)S(1)} %sub.237, pred[512,1536]{0,1:T(8,128)(4,1)S(1)} %fusion.135, bf16[2560,4,128]{0,2,1:T(8,128)(2,1)} %get-tuple-element.1022, s32[]{:T(128)S(6)} %select_n.92), kind=kOutput, calls=%fused_computation.41.clone.1 | convolution fusion | flops 1629487104 | bytes 28590084 | tf_op jit(solution)/shard_map/while/body/eval_jaxpr/rkgd,ckd->kgrc/dot_general | solution.py:27
  187.8 14.9 %fusion.137 = bf16[4,2,512,1536]{2,3,1,0:T(8,128)(2,1)} fusion(f32[4,2,512,1536]{2,3,1,0:T(8,128)} %fusion.136, bf16[512,4,2,128]{0,3,2,1:T(8,128)(2,1)S(1)} %bitcast.281, f32[4,2,512]{2,1,0:T(2,128)S(1)} %sub.239, bf16[2560,4,128]{0,2,1:T(8,128)(2,1)} %get-tuple-element.1027, s32[]{:T(128)S(6)} %select_n.92), kind=kOutput, calls=%fused_computation.38.clone.1 | convolution fusion | flops 1629487104 | bytes 40386564 | tf_op jit(solution)/shard_map/while/body/eval_jaxpr/rkgd,ckd->kgrc/dot_general | solution.py:39
  222.0 15.0 %fusion.138 = f32[2560,4,128]{0,2,1:T(8,128)} fusion(f32[2560,4,128]{0,2,1:T(8,128)} %get-tuple-element.1003, s32[]{:T(128)S(6)} %select_n.92, bf16[512,4,2,128]{0,3,2,1:T(8,128)(2,1)S(1)} %bitcast.282, f32[4,2,512,1536]{2,3,1,0:T(8,128)} %fusion.136), kind=kOutput, calls=%fused_computation.47.clone.1 | convolution fusion | flops 1617690624 | bytes 32505860 | tf_op jit(solution)/shard_map/while/body/eval_jaxpr/kgrc,rkgd->ckd/dot_general | solution.py:42
  240.7 13.0 %fusion.136 = f32[4,2,512,1536]{2,3,1,0:T(8,128)} fusion(bf16[512,4,2,128]{0,3,2,1:T(8,128)(2,1)S(1)} %bitcast.289, f32[4,2,512]{2,1,0:T(2,128)S(1)} %sub.237, pred[512,1536]{0,1:T(8,128)(4,1)S(1)} %fusion.135, bf16[2560,4,128]{0,2,1:T(8,128)(2,1)} %get-tuple-element.1022, s32[]{:T(128)S(6)} %select_n.92), kind=kOutput, calls=%fused_computation.41.clone.1 | convolution fusion | flops 1629487104 | bytes 28590084 | tf_op jit(solution)/shard_map/while/body/eval_jaxpr/rkgd,ckd->kgrc/dot_general | solution.py:27
  253.7 14.9 %fusion.137 = bf16[4,2,512,1536]{2,3,1,0:T(8,128)(2,1)} fusion(f32[4,2,512,1536]{2,3,1,0:T(8,128)} %fusion.136, bf16[512,4,2,128]{0,3,2,1:T(8,128)(2,1)S(1)} %bitcast.281, f32[4,2,512]{2,1,0:T(2,128)S(1)} %sub.239, bf16[2560,4,128]{0,2,1:T(8,128)(2,1)} %get-tuple-element.1027, s32[]{:T(128)S(6)} %select_n.92), kind=kOutput, calls=%fused_computation.38.clone.1 | convolution fusion | flops 1629487104 | bytes 40386564 | tf_op jit(solution)/shard_map/while/body/eval_jaxpr/rkgd,ckd->kgrc/dot_general | solution.py:39
  287.9 15.1 %fusion.138 = f32[2560,4,128]{0,2,1:T(8,128)} fusion(f32[2560,4,128]{0,2,1:T(8,128)} %get-tuple-element.1003, s32[]{:T(128)S(6)} %select_n.92, bf16[512,4,2,128]{0,3,2,1:T(8,128)(2,1)S(1)} %bitcast.282, f32[4,2,512,1536]{2,3,1,0:T(8,128)} %fusion.136), kind=kOutput, calls=%fused_computation.47.clone.1 | convolution fusion | flops 1617690624 | bytes 32505860 | tf_op jit(solution)/shard_map/while/body/eval_jaxpr/kgrc,rkgd->ckd/dot_general | solution.py:42
  315.2 200.9 %while.42 = (s32[]{:T(128)}, bf16[1536,8,128]{0,2,1:T(8,128)(2,1)}, f32[2560,4,128]{0,2,1:T(8,128)}, f32[2560,4,128]{0,2,1:T(8,128)}, bf16[2560,4,128]{0,2,1:T(8...) while((s32[]{:T(128)}, bf16[1536,8,128]{0,2,1:T(8,128)(2,1)}, ...), condition=%wide.region_2.3_spmd, body=%wide.region_1.2_spmd.sunk | while | flops 8104449024 | bytes 143838512 | solution.py:91
  319.9 13.1 %fusion.122 = f32[4,2,512,1536]{2,3,1,0:T(8,128)} fusion(bf16[512,4,2,128]{0,3,2,1:T(8,128)(2,1)S(1)} %bitcast.291, f32[4,2,512]{2,1,0:T(2,128)S(1)} %sub.229, pred[512,1536]{0,1:T(8,128)(4,1)S(1)} %fusion.121, bf16[2560,4,128]{0,2,1:T(8,128)(2,1)} %get-tuple-element.1076, s32[]{:T(128)S(6)} %select_n.89), kind=kOutput, calls=%fused_computation.5.clone.1 | convolution fusion | flops 1629487104 | bytes 28590084 | tf_op jit(solution)/shard_map/while/body/eval_jaxpr/rkgd,ckd->kgrc/dot_general | solution.py:27
  333.0 15.0 %fusion.123 = bf16[4,2,512,1536]{2,3,1,0:T(8,128)(2,1)} fusion(f32[4,2,512,1536]{2,3,1,0:T(8,128)} %fusion.122, bf16[512,4,2,128]{0,3,2,1:T(8,128)(2,1)S(1)} %bitcast.283, f32[4,2,512]{2,1,0:T(2,128)S(1)} %sub.231, bf16[2560,4,128]{0,2,1:T(8,128)(2,1)} %get-tuple-element.1081, s32[]{:T(128)S(6)} %select_n.89), kind=kOutput, calls=%fused_computation.2.clone.1 | convolution fusion | flops 1629487104 | bytes 40386564 | tf_op jit(solution)/shard_map/while/body/eval_jaxpr/rkgd,ckd->kgrc/dot_general | solution.py:39
  367.2 15.1 %fusion.124 = f32[2560,4,128]{0,2,1:T(8,128)} fusion(f32[2560,4,128]{0,2,1:T(8,128)} %get-tuple-element.1057, s32[]{:T(128)S(6)} %select_n.89, bf16[512,4,2,128]{0,3,2,1:T(8,128)(2,1)S(1)} %bitcast.284, f32[4,2,512,1536]{2,3,1,0:T(8,128)} %fusion.122), kind=kOutput, calls=%fused_computation.11.clone.1 | convolution fusion | flops 1617690624 | bytes 32505860 | tf_op jit(solution)/shard_map/while/body/eval_jaxpr/kgrc,rkgd->ckd/dot_general | solution.py:42
  386.6 13.1 %fusion.122 = f32[4,2,512,1536]{2,3,1,0:T(8,128)} fusion(bf16[512,4,2,128]{0,3,2,1:T(8,128)(2,1)S(1)} %bitcast.291, f32[4,2,512]{2,1,0:T(2,128)S(1)} %sub.229, pred[512,1536]{0,1:T(8,128)(4,1)S(1)} %fusion.121, bf16[2560,4,128]{0,2,1:T(8,128)(2,1)} %get-tuple-element.1076, s32[]{:T(128)S(6)} %select_n.89), kind=kOutput, calls=%fused_computation.5.clone.1 | convolution fusion | flops 1629487104 | bytes 28590084 | tf_op jit(solution)/shard_map/while/body/eval_jaxpr/rkgd,ckd->kgrc/dot_general | solution.py:27
  399.7 15.0 %fusion.123 = bf16[4,2,512,1536]{2,3,1,0:T(8,128)(2,1)} fusion(f32[4,2,512,1536]{2,3,1,0:T(8,128)} %fusion.122, bf16[512,4,2,128]{0,3,2,1:T(8,128)(2,1)S(1)} %bitcast.283, f32[4,2,512]{2,1,0:T(2,128)S(1)} %sub.231, bf16[2560,4,128]{0,2,1:T(8,128)(2,1)} %get-tuple-element.1081, s32[]{:T(128)S(6)} %select_n.89), kind=kOutput, calls=%fused_computation.2.clone.1 | convolution fusion | flops 1629487104 | bytes 40386564 | tf_op jit(solution)/shard_map/while/body/eval_jaxpr/rkgd,ckd->kgrc/dot_general | solution.py:39
  433.9 15.1 %fusion.124 = f32[2560,4,128]{0,2,1:T(8,128)} fusion(f32[2560,4,128]{0,2,1:T(8,128)} %get-tuple-element.1057, s32[]{:T(128)S(6)} %select_n.89, bf16[512,4,2,128]{0,3,2,1:T(8,128)(2,1)S(1)} %bitcast.284, f32[4,2,512,1536]{2,3,1,0:T(8,128)} %fusion.122), kind=kOutput, calls=%fused_computation.11.clone.1 | convolution fusion | flops 1617690624 | bytes 32505860 | tf_op jit(solution)/shard_map/while/body/eval_jaxpr/kgrc,rkgd->ckd/dot_general | solution.py:42
  453.3 13.1 %fusion.122 = f32[4,2,512,1536]{2,3,1,0:T(8,128)} fusion(bf16[512,4,2,128]{0,3,2,1:T(8,128)(2,1)S(1)} %bitcast.291, f32[4,2,512]{2,1,0:T(2,128)S(1)} %sub.229, pred[512,1536]{0,1:T(8,128)(4,1)S(1)} %fusion.121, bf16[2560,4,128]{0,2,1:T(8,128)(2,1)} %get-tuple-element.1076, s32[]{:T(128)S(6)} %select_n.89), kind=kOutput, calls=%fused_computation.5.clone.1 | convolution fusion | flops 1629487104 | bytes 28590084 | tf_op jit(solution)/shard_map/while/body/eval_jaxpr/rkgd,ckd->kgrc/dot_general | solution.py:27
  466.4 15.0 %fusion.123 = bf16[4,2,512,1536]{2,3,1,0:T(8,128)(2,1)} fusion(f32[4,2,512,1536]{2,3,1,0:T(8,128)} %fusion.122, bf16[512,4,2,128]{0,3,2,1:T(8,128)(2,1)S(1)} %bitcast.283, f32[4,2,512]{2,1,0:T(2,128)S(1)} %sub.231, bf16[2560,4,128]{0,2,1:T(8,128)(2,1)} %get-tuple-element.1081, s32[]{:T(128)S(6)} %select_n.89), kind=kOutput, calls=%fused_computation.2.clone.1 | convolution fusion | flops 1629487104 | bytes 40386564 | tf_op jit(solution)/shard_map/while/body/eval_jaxpr/rkgd,ckd->kgrc/dot_general | solution.py:39
  500.6 15.3 %fusion.124 = f32[2560,4,128]{0,2,1:T(8,128)} fusion(f32[2560,4,128]{0,2,1:T(8,128)} %get-tuple-element.1057, s32[]{:T(128)S(6)} %select_n.89, bf16[512,4,2,128]{0,3,2,1:T(8,128)(2,1)S(1)} %bitcast.284, f32[4,2,512,1536]{2,3,1,0:T(8,128)} %fusion.122), kind=kOutput, calls=%fused_computation.11.clone.1 | convolution fusion | flops 1617690624 | bytes 32505860 | tf_op jit(solution)/shard_map/while/body/eval_jaxpr/kgrc,rkgd->ckd/dot_general | solution.py:42
  529.2 16.3 %copy.179 = bf16[2,1536,1024]{2,0,1:T(2,128)(2,1)} copy(bf16[2,1536,1024]{1,2,0:T(8,128)(2,1)} %pad_maximum_fusion) | data formatting | bytes 12582912 | tf_op jit(solution)/shard_map/stack | solution.py:163
  559.4 12.8 %collective-permute-done.2 = f32[2,1024,4,128]{1,3,2,0:T(8,128)} collective-permute-done((f32[2,1024,4,128]{1,3,2,0:T(8,128)}, f32[2,1024,4,128]{1,3,2,0:T(8,128)}, u32[]{:S(2)}, u32[]{:S(2)}) %collective-permute-start.2) | collective-permute-done | bytes 4194336 | tf_op jit(solution)/shard_map/ppermute | solution.py:16
  582.0 39.9 %all-to-all-done = bf16[2,1536,1024]{2,0,1:T(2,128)(2,1)} async-done(((bf16[2,1536,1024]{2,0,1:T(2,128)(2,1)}), bf16[2,1536,1024]{2,0,1:T(2,128)(2,1)}, u32[]{:S(2)}, u32[]{:S(2)}) %all-to-all-start) | async-done | bytes 6291488 | tf_op jit(solution)/shard_map/all_to_all | solution.py:181
  647.2 14.8 %all-to-all-done.1 = bf16[2,1536,512]{2,0,1:T(2,128)(2,1)S(1)} async-done(((bf16[2,1536,512]{2,0,1:T(2,128)(2,1)}), bf16[2,1536,512]{2,0,1:T(2,128)(2,1)S(1)}, u32[]{:S(2)}, u32[]{:S(2)}) %all-to-all-start.1) | async-done | bytes 3145760 | tf_op jit(solution)/shard_map/all_to_all | solution.py:182
  (172 shorter events, 368.0 us)
Async XLA Ops:
  0.6 1.6 slice-start.6
  4.7 2.1 slice-start.7
  4.7 84.1 %collective-permute-start = (bf16[2,1024,512]{1,2,0:T(8,128)(2,1)}, bf16[2,1024,512]{1,2,0:T(8,128)(2,1)}, u32[]{:S(2)}, u32[]{:S(2)}) collective-permute-start(bf16[2,1024,512]{1,2,0:T(8,128)(2,1)} %copy.223), channel_id=1, source_target_pairs={{0,4},{4,8},{8,12},{12,16},{16,20},{20,24},{24,28},{1,5},{5,9},{9,... | collective-permute-start | bytes 6291464 | tf_op jit(solution)/shard_map/ppermute | solution.py:16
  9.3 82.3 %collective-permute-start.1 = (bf16[2,1024,512]{1,2,0:T(8,128)(2,1)}, bf16[2,1024,512]{1,2,0:T(8,128)(2,1)}, u32[]{:S(2)}, u32[]{:S(2)}) collective-permute-start(bf16[2,1024,512]{1,2,0:T(8,128)(2,1)} %copy.226), channel_id=1, source_target_pairs={{0,4},{4,8},{8,12},{12,16},{16,20},{20,24},{24,28},{1,5},{5,9},{9,... | collective-permute-start | bytes 6291464 | tf_op jit(solution)/shard_map/ppermute | solution.py:16
  11.2 10.4 %slice-start.4 = ((s8[6291456]{0:T(1024)(128)(4,1)}), s8[4194304]{0:T(1024)(128)(4,1)S(1)}, s32[]{:S(2)}) async-start(s8[6291456]{0:T(1024)(128)(4,1)} %bitcast.299), calls=%async_computation.7 | async-start | bytes 8388608
  15.3 6.4 slice-start.5
  39.4 6.0 copy-start.1
  73.7 5.4 copy-start
  82.0 4.7 copy-start.6
  82.0 5.6 copy-start.8
  82.0 6.2 copy-start.7
  91.6 3.0 copy-start.4
  91.6 3.0 copy-start.5
  519.5 6.4 copy-start.2
  519.5 6.4 copy-start.3
  522.0 50.2 %collective-permute-start.2 = (f32[2,1024,4,128]{1,3,2,0:T(8,128)}, f32[2,1024,4,128]{1,3,2,0:T(8,128)}, u32[]{:S(2)}, u32[]{:S(2)}) collective-permute-start(f32[2,1024,4,128]{1,3,2,0:T(8,128)} %pad_maximum_fusion.1), channel_id=1, source_target_pairs={{4,0},{8,4},{12,8},{16,12},{20,16},{24,20},{28,24},{5,1},{9,5},{13... | collective-permute-start | bytes 12582920 | tf_op jit(solution)/shard_map/ppermute | solution.py:16
  545.5 26.7 %slice-start.2 = ((s8[5242880]{0:T(1024)(128)(4,1)}), s8[1048576]{0:T(1024)(128)(4,1)S(1)}, s32[]{:S(2)}) async-start(s8[5242880]{0:T(1024)(128)(4,1)} %bitcast.287), calls=%async_computation.5 | async-start | bytes 2097152
  545.5 76.4 %all-to-all-start = ((bf16[2,1536,1024]{2,0,1:T(2,128)(2,1)}), bf16[2,1536,1024]{2,0,1:T(2,128)(2,1)}, u32[]{:S(2)}, u32[]{:S(2)}) async-start(bf16[2,1536,1024]{2,0,1:T(2,128)(2,1)} %copy.179), calls=%async_computation | async-start | bytes 12582912 | tf_op jit(solution)/shard_map/all_to_all | solution.py:181
  550.9 21.3 %slice-start.3 = ((s8[5242880]{0:T(1024)(128)(4,1)}), s8[4194304]{0:T(1024)(128)(4,1)S(1)}, s32[]{:S(2)}) async-start(s8[5242880]{0:T(1024)(128)(4,1)} %bitcast.287), calls=%async_computation.6 | async-start | bytes 8388608
  552.8 19.4 %slice-start = ((s8[5242880]{0:T(1024)(128)(4,1)}), s8[4194304]{0:T(1024)(128)(4,1)S(1)}, s32[]{:S(2)}) async-start(s8[5242880]{0:T(1024)(128)(4,1)} %bitcast.285), calls=%async_computation.3 | async-start | bytes 8388608
  554.7 17.6 %slice-start.1 = ((s8[5242880]{0:T(1024)(128)(4,1)}), s8[1048576]{0:T(1024)(128)(4,1)S(1)}, s32[]{:S(2)}) async-start(s8[5242880]{0:T(1024)(128)(4,1)} %bitcast.285), calls=%async_computation.4 | async-start | bytes 2097152
  557.0 68.6 %collective-permute-start.3 = (f32[2,1024,4,128]{1,3,2,0:T(8,128)}, f32[2,1024,4,128]{1,3,2,0:T(8,128)}, u32[]{:S(2)}, u32[]{:S(2)}) collective-permute-start(f32[2,1024,4,128]{1,3,2,0:T(8,128)} %pad_maximum_fusion.2), channel_id=1, source_target_pairs={{4,0},{8,4},{12,8},{16,12},{20,16},{24,20},{28,24},{5,1},{9,5},{13... | collective-permute-start | bytes 12582920 | tf_op jit(solution)/shard_map/ppermute | solution.py:16
  621.9 40.1 %all-to-all-start.1 = ((bf16[2,1536,512]{2,0,1:T(2,128)(2,1)}), bf16[2,1536,512]{2,0,1:T(2,128)(2,1)S(1)}, u32[]{:S(2)}, u32[]{:S(2)}) async-start(bf16[2,1536,512]{2,0,1:T(2,128)(2,1)} %copy.182), calls=%async_computation.1 | async-start | bytes 6291456 | tf_op jit(solution)/shard_map/all_to_all | solution.py:182
  662.0 40.3 %all-to-all-start.2 = ((bf16[2,1536,512]{2,0,1:T(2,128)(2,1)}), bf16[2,1536,512]{2,0,1:T(2,128)(2,1)}, u32[]{:S(2)}, u32[]{:S(2)}) async-start(bf16[2,1536,512]{2,0,1:T(2,128)(2,1)} %copy.185), calls=%async_computation.2 | async-start | bytes 6291456 | tf_op jit(solution)/shard_map/all_to_all | solution.py:183
where the time goes:
time: 722 us; the launch traced here: 712 us
  matrix products  367 us (51%)
  local copies, waits for them, and re-layouts  193 us (27%)
  waiting for transfers between devices  69.9 us (10%)
  other arithmetic  55.8 us (8%)
  starting transfers between devices  24 us (3%)
    dot_general x6, matrix products, block_grads(): jnp.einsum('kgrc,rkgd->ckd', prob_low, do_heads, preferred_element_type=j...  90.6 us
    dot_general x6, matrix products, block_grads(): jnp.einsum('rkgd,ckd->kgrc', do_heads, v_block, preferred_element_type=jn...  89.5 us
    dot_general x6, matrix products, block_grads(): jnp.einsum('rkgd,ckd->kgrc', query_head_count, k_block, preferred_element...  78.2 us
    dot_general x6, matrix products, block_grads(): jnp.einsum('kgrc,rkgd->ckd', score_low, query_head_count, preferred_eleme...  68 us
    unnamed x44, local copies, waits for them, and re-layouts  60 us
    dot_general x6, matrix products, block_grads(): jnp.einsum('kgrc,ckd->rkgd', score_low, k_block, preferred_element_type=j...  41.2 us
    all_to_all x1, waiting for transfers between devices, shards(): lax.all_to_all(dq_stack, 'head', split_axis=1, concat_axis=2, tiled=True)  39.9 us
    another operation x1, local copies, waits for them, and re-layouts, shards(): jnp.stack([entry[0].reshape(tok_local, head_local * HEAD_SIZE) for entry...  16.3 us
  transfers between devices with their start and end apart: 7, of which 4 were waited for; matrix products, arithmetic and copies ran while one was open for 24% of the time, Pallas kernels for 0%

commit v1 on v0

v1 whole, which is shorter than its diff:
```python
import functools
import math

import jax
import jax.numpy as jnp
from jax import lax
from jax.experimental import pallas as pl
from jax.experimental.pallas import tpu as pltpu
from jax.sharding import PartitionSpec as P

HEAD_SIZE = 128
WINDOW_LENGTH = 1024
QUERY_PRE = 168
SLIDING_LAYERS = 2
TILE = 256
SCALE = QUERY_PRE ** (-0.5)
LOG2E = math.log2(math.e)
FAR = 1 << 20

NT = (((1,), (1,)), ((), ()))
NN = (((1,), (0,)), ((), ()))


def dot(a, b, dims=NN):
    return lax.dot_general(a, b, dims, preferred_element_type=jnp.float32)


def shifted(value, axis, steps):
    count = lax.axis_size(axis)
    first, last = (max(0, -steps), min(count, count - steps))
    return lax.ppermute(value, axis, [(source, source + steps) for source in range(first, last)])


def swapped(value, axis, flip):
    count = lax.axis_size(axis)
    return lax.ppermute(value, axis, [(source, source ^ flip) for source in range(count)])


def band_kernel(
    layer, kv_first, kv_count, owners, scal, q_ref, do_ref, out_ref, lse_ref, k_ref, v_ref, halo_ref, *rest
):
    dq_bufs = rest[:owners]
    back_ref, part_ref, kx, vx, kt, acc, dq_scr, sems = rest[owners:]
    tok_local = q_ref.shape[1]
    group = q_ref.shape[2] // HEAD_SIZE
    chunk = tok_local // owners
    step = pl.program_id(0)
    me = scal[0]
    first_shard = scal[1]
    win = scal[2 + layer]
    wide = group * TILE

    kx[0:WINDOW_LENGTH] = halo_ref[:, 0:HEAD_SIZE]
    vx[0:WINDOW_LENGTH] = halo_ref[:, HEAD_SIZE : 2 * HEAD_SIZE]
    kx[WINDOW_LENGTH:] = k_ref[0]
    vx[WINDOW_LENGTH:] = v_ref[0]
    kt[...] = kx[...].T
    acc[...] = jnp.zeros_like(acc)

    rows = lax.broadcasted_iota(jnp.int32, (TILE, wide), 0)
    lanes = lax.broadcasted_iota(jnp.int32, (1, wide), 1) % TILE

    def stacked(ref, start):
        block = ref[0, pl.ds(start, TILE), :]
        return jnp.concatenate(
            [block[:, h * HEAD_SIZE : (h + 1) * HEAD_SIZE] for h in range(group)], 0
        )

    def one_block(block, carry):
        start = pl.multiple_of(block * TILE, TILE)
        q2 = stacked(q_ref, start)
        do2 = stacked(do_ref, start)
        prod = do2.astype(jnp.float32) * stacked(out_ref, start).astype(jnp.float32)
        high = prod.astype(jnp.bfloat16)
        low = (prod - high.astype(jnp.float32)).astype(jnp.bfloat16)
        ones = jnp.ones((8, HEAD_SIZE), jnp.bfloat16)
        delta = (dot(ones, high, NT) + dot(ones, low, NT))[0:1]
        head = (kv_first + step) * group
        lse = jnp.concatenate(
            [lse_ref[0, pl.ds(head + h, 1), pl.ds(start, TILE)] for h in range(group)], 1
        )
        lse2 = lse * LOG2E
        dq_t = jnp.zeros((HEAD_SIZE, wide), jnp.float32)
        tiles = WINDOW_LENGTH // TILE + 1
        for tile in range(tiles):
            begin = pl.multiple_of(start + tile * TILE, TILE)
            span = pl.ds(begin, TILE)
            scores = dot(kx[span, :], q2, NT)
            prob = jnp.exp2(scores * (SCALE * LOG2E) - lse2)
            if tile == tiles - 1:
                seen = rows <= lanes
            else:
                bound = WINDOW_LENGTH - win - tile * TILE
                outside = jnp.logical_and(first_shard == 1, begin < WINDOW_LENGTH)
                seen = rows > lanes + jnp.where(outside, FAR, bound)
            prob = jnp.where(seen, prob, 0.0)
            grad_prob = dot(vx[span, :], do2, NT)
            grad_score = prob * (grad_prob - delta)
            prob_low = prob.astype(jnp.bfloat16)
            score_low = grad_score.astype(jnp.bfloat16)
            acc[span, HEAD_SIZE:] += dot(prob_low, do2)
            acc[span, :HEAD_SIZE] += dot(score_low, q2)
            dq_t += dot(kt[:, span], score_low)
        dq = (dq_t.T * SCALE).astype(jnp.bfloat16)
        for h in range(group):
            dq_scr[step, pl.ds(start, TILE), h * HEAD_SIZE : (h + 1) * HEAD_SIZE] = dq[
                h * TILE : (h + 1) * TILE
            ]
        return carry

    lax.fori_loop(0, tok_local // TILE, one_block, 0)

    back_ref[:, :HEAD_SIZE] = (acc[0:WINDOW_LENGTH, :HEAD_SIZE] * SCALE).astype(jnp.bfloat16)
    back_ref[:, HEAD_SIZE:] = acc[0:WINDOW_LENGTH, HEAD_SIZE:].astype(jnp.bfloat16)
    part_ref[:, :HEAD_SIZE] = acc[WINDOW_LENGTH:, :HEAD_SIZE] * SCALE
    part_ref[:, HEAD_SIZE:] = acc[WINDOW_LENGTH:, HEAD_SIZE:]

    def copies(index):
        result = []
        for flip in range(owners):
            owner = jnp.bitwise_xor(me, flip)
            source = dq_scr.at[index, pl.ds(pl.multiple_of(owner * chunk, chunk), chunk), :]
            target = dq_bufs[flip].at[:, pl.ds(index * group * HEAD_SIZE, group * HEAD_SIZE)]
            result.append(pltpu.make_async_copy(source, target, sems.at[index, flip]))
        return result

    for index in range(kv_count):

        @pl.when(step == index)
        def _(index=index):
            for copy in copies(index):
                copy.start()

    @pl.when(step == kv_count - 1)
    def _():
        for index in range(kv_count):
            for copy in copies(index):
                copy.wait()


def band_call(piece, extra, owners, scal, queries, grad_out, attn_out, log_norm, keys, values, halo):
    layer, kv_first, kv_count = piece
    tok_local = queries.shape[1]
    group = queries.shape[2] // keys.shape[2]
    span = WINDOW_LENGTH + tok_local
    chunk = tok_local // owners
    q_spec = pl.BlockSpec((1, tok_local, group * HEAD_SIZE), lambda g: (layer, 0, kv_first + g))
    kv_spec = pl.BlockSpec((1, tok_local, HEAD_SIZE), lambda g: (layer, 0, kv_first + g))
    pairs = tok_local * (WINDOW_LENGTH + TILE) * group * kv_count
    outs = pl.pallas_call(
        functools.partial(band_kernel, layer, kv_first, kv_count, owners),
        grid=(kv_count,),
        in_specs=[
            pl.BlockSpec(memory_space=pltpu.SMEM),
            q_spec,
            q_spec,
            q_spec,
            pl.BlockSpec((1,) + log_norm.shape[1:], lambda g: (layer, 0, 0)),
            kv_spec,
            kv_spec,
            pl.BlockSpec((WINDOW_LENGTH, 2 * HEAD_SIZE), lambda g: (0, g)),
        ],
        out_specs=[pl.BlockSpec(memory_space=pl.ANY)] * owners
        + [
            pl.BlockSpec((WINDOW_LENGTH, 2 * HEAD_SIZE), lambda g: (0, g)),
            pl.BlockSpec((tok_local, 2 * HEAD_SIZE), lambda g: (0, g)),
        ],
        out_shape=[
            jax.ShapeDtypeStruct((chunk, (kv_count * group + extra) * HEAD_SIZE), jnp.bfloat16)
        ]
        * owners
        + [
            jax.ShapeDtypeStruct((WINDOW_LENGTH, kv_count * 2 * HEAD_SIZE), jnp.bfloat16),
            jax.ShapeDtypeStruct((tok_local, kv_count * 2 * HEAD_SIZE), jnp.float32),
        ],
        scratch_shapes=[
            pltpu.VMEM((span, HEAD_SIZE), jnp.bfloat16),
            pltpu.VMEM((span, HEAD_SIZE), jnp.bfloat16),
            pltpu.VMEM((HEAD_SIZE, span), jnp.bfloat16),
            pltpu.VMEM((span, 2 * HEAD_SIZE), jnp.float32),
            pltpu.VMEM((kv_count, tok_local, group * HEAD_SIZE), jnp.bfloat16),
            pltpu.SemaphoreType.DMA((kv_count, owners)),
        ],
        compiler_params=pltpu.CompilerParams(vmem_limit_bytes=40 * 1024 * 1024),
        cost_estimate=pl.CostEstimate(
            flops=pairs * 2 * HEAD_SIZE * 5 * 2,
            bytes_accessed=8 * tok_local * group * kv_count * HEAD_SIZE,
            transcendentals=pairs,
        ),
        name="band",
    )(scal, queries, grad_out, attn_out, log_norm, keys, values, halo)
    return outs[:owners], outs[owners], outs[owners + 1]


def finish_kernel(kv_count, owners, column, aliased, scal, part_ref, back_ref, *rest):
    bufs = rest[owners if aliased else 0 :][:owners]
    scr, sems = rest[-2:]
    tok_local = part_ref.shape[0]
    chunk = tok_local // owners
    step = pl.program_id(0)
    me = scal[0]
    plain = tok_local - WINDOW_LENGTH
    scr[step, :plain] = part_ref[:plain].astype(jnp.bfloat16)
    scr[step, plain:] = (part_ref[plain:] + back_ref[...].astype(jnp.float32)).astype(jnp.bfloat16)

    def copies(index):
        result = []
        for flip in range(owners):
            owner = jnp.bitwise_xor(me, flip)
            rows = pl.ds(pl.multiple_of(owner * chunk, chunk), chunk)
            for kind in range(2):
                place = column + (kind * kv_count + index) * HEAD_SIZE
                result.append(
                    pltpu.make_async_copy(
                        scr.at[index, rows, pl.ds(kind * HEAD_SIZE, HEAD_SIZE)],
                        bufs[flip].at[:, pl.ds(place, HEAD_SIZE)],
                        sems.at[index, flip, kind],
                    )
                )
        return result

    for index in range(kv_count):

        @pl.when(step == index)
        def _(index=index):
            for copy in copies(index):
                copy.start()

    @pl.when(step == kv_count - 1)
    def _():
        for index in range(kv_count):
            for copy in copies(index):
                copy.wait()


def finish_call(kv_count, owners, column, scal, part, back, bufs):
    tok_local = part.shape[0]
    chunk = tok_local // owners
    aliased = bufs is not None
    shape = jax.ShapeDtypeStruct((chunk, column + kv_count * 2 * HEAD_SIZE), jnp.bfloat16)
    any_spec = pl.BlockSpec(memory_space=pl.ANY)
    return pl.pallas_call(
        functools.partial(finish_kernel, kv_count, owners, column, aliased),
        grid=(kv_count,),
        in_specs=[
            pl.BlockSpec(memory_space=pltpu.SMEM),
            pl.BlockSpec((tok_local, 2 * HEAD_SIZE), lambda g: (0, g)),
            pl.BlockSpec((WINDOW_LENGTH, 2 * HEAD_SIZE), lambda g: (0, g)),
        ]
        + ([any_spec] * owners if aliased else []),
        out_specs=[any_spec] * owners,
        out_shape=[shape] * owners,
        input_output_aliases={3 + i: i for i in range(owners)} if aliased else {},
        scratch_shapes=[
            pltpu.VMEM((kv_count, tok_local, 2 * HEAD_SIZE), jnp.bfloat16),
            pltpu.SemaphoreType.DMA((kv_count, owners, 2)),
        ],
        compiler_params=pltpu.CompilerParams(vmem_limit_bytes=32 * 1024 * 1024),
        cost_estimate=pl.CostEstimate(
            flops=0, bytes_accessed=16 * tok_local * kv_count * HEAD_SIZE, transcendentals=0
        ),
        name="finish",
    )(scal, part, back, *(bufs if aliased else ()))


def place_kernel(plan, owners, group, kv_local, aliased, scal, *rest):
    blocks = rest[:owners]
    outs = rest[owners + (3 if aliased else 0) :][:3]
    sems = rest[-1]
    me = scal[0]
    copies = []
    for flip in range(owners):
        source = jnp.bitwise_xor(me, flip)
        column = 0
        for which, (layer, kv_first, kv_count) in plan:
            heads = kv_count * group if which == 0 else kv_count
            home = kv_local * group if which == 0 else kv_local
            first = kv_first * group if which == 0 else kv_first
            place = pl.multiple_of((source * home + first) * HEAD_SIZE, HEAD_SIZE)
            copies.append(
                pltpu.make_async_copy(
                    blocks[flip].at[:, pl.ds(column, heads * HEAD_SIZE)],
                    outs[which].at[layer, :, pl.ds(place, heads * HEAD_SIZE)],
                    sems.at[len(copies)],
                )
            )
            column += heads * HEAD_SIZE
    for copy in copies:
        copy.start()
    for copy in copies:
        copy.wait()


def place_call(plan, owners, group, kv_local, scal, blocks, outs):
    chunk, width = blocks[0].shape
    aliased = outs is not None
    any_spec = pl.BlockSpec(memory_space=pl.ANY)
    shapes = [
        jax.ShapeDtypeStruct(
            (SLIDING_LAYERS, chunk, owners * heads * HEAD_SIZE), jnp.bfloat16
        )
        for heads in (kv_local * group, kv_local, kv_local)
    ]
    return pl.pallas_call(
        functools.partial(place_kernel, plan, owners, group, kv_local, aliased),
        in_specs=[pl.BlockSpec(memory_space=pltpu.SMEM)]
        + [any_spec] * (owners + (3 if aliased else 0)),
        out_specs=[any_spec] * 3,
        out_shape=shapes,
        input_output_aliases={1 + owners + i: i for i in range(3)} if aliased else {},
        scratch_shapes=[pltpu.SemaphoreType.DMA((owners * len(plan),))],
        cost_estimate=pl.CostEstimate(
            flops=0, bytes_accessed=owners * chunk * width * 4, transcendentals=0
        ),
        name="place",
    )(scal, *blocks, *(outs if aliased else ()))


def shards(queries, layer_keys_input, layer_values_input, attn_out, grad_out, log_norm, window):
    tok_local = queries.shape[1]
    kv_local = layer_keys_input.shape[2] // HEAD_SIZE
    group = queries.shape[2] // layer_keys_input.shape[2]
    owners = lax.axis_size("head")
    shard = lax.axis_index("ctx")
    scal = jnp.concatenate(
        [
            jnp.stack([lax.axis_index("head"), (shard == 0).astype(jnp.int32)]).astype(jnp.int32),
            window.astype(jnp.int32),
        ]
    )
    each = min(2, kv_local)
    pieces = [
        (layer, kv_first, each)
        for layer in range(SLIDING_LAYERS)
        for kv_first in range(0, kv_local, each)
    ]

    halos = []
    for layer, kv_first, kv_count in pieces:
        parts = []
        for kv in range(kv_first, kv_first + kv_count):
            columns = slice(kv * HEAD_SIZE, (kv + 1) * HEAD_SIZE)
            parts.append(layer_keys_input[layer, tok_local - WINDOW_LENGTH :, columns])
            parts.append(layer_values_input[layer, tok_local - WINDOW_LENGTH :, columns])
        halos.append(shifted(jnp.concatenate(parts, 1), "ctx", 1))

    outs = None
    waiting = None

    def send(plan, bufs, outs):
        blocks = [bufs[0]] + [swapped(bufs[flip], "head", flip) for flip in range(1, owners)]
        return place_call(plan, owners, group, kv_local, scal, blocks, outs)

    for piece, halo in zip(pieces, halos):
        kv_count = piece[2]
        extra = 0 if waiting is None else 2 * waiting[0][2]
        bufs, back, part = band_call(
            piece,
            extra,
            owners,
            scal,
            queries,
            grad_out,
            attn_out,
            log_norm,
            layer_keys_input,
            layer_values_input,
            halo,
        )
        back = shifted(back, "ctx", -1)
        plan = [(0, piece)]
        if waiting is not None:
            old, old_part, old_back = waiting
            bufs = finish_call(
                old[2], owners, kv_count * group * HEAD_SIZE, scal, old_part, old_back, bufs
            )
            plan += [(1, old), (2, old)]
        outs = send(plan, bufs, outs)
        waiting = (piece, part, back)
    old, old_part, old_back = waiting
    bufs = finish_call(old[2], owners, 0, scal, old_part, old_back, None)
    outs = send([(1, old), (2, old)], bufs, outs)
    return tuple(outs)


def solution(mesh):
    in_specs = (
        P(None, "ctx", "head"),
        P(None, "ctx", "head"),
        P(None, "ctx", "head"),
        P(None, "ctx", "head"),
        P(None, "ctx", "head"),
        P(None, "head", "ctx"),
        P(),
    )
    out_specs = (
        P(None, ("ctx", "head"), None),
        P(None, ("ctx", "head"), None),
        P(None, ("ctx", "head"), None),
    )
    return jax.shard_map(shards, mesh=mesh, in_specs=in_specs, out_specs=out_specs, check_vma=False)
```

time: 722 us -> 654 us (0.906); the launches traced: 712 us -> 653 us
  Pallas kernels: 0 us -> 524 us
  matrix products: 367 us -> 0 us
  local copies, waits for them, and re-layouts: 193 us -> 11.6 us
  other arithmetic: 55.8 us -> 4.41 us
  starting transfers between devices: 24 us -> 35.5 us
    pallas_call x0 -> x13, Pallas kernels: none -> 524 us  [the longest x5 390 us: place_call(): pl.pallas_call(functools.partial(place_kernel, plan, owners, group, kv_lo...]
    dot_general x30 -> x0, matrix products: 367 us -> none  [the longest x6 90.6 us: block_grads(): jnp.einsum('kgrc,rkgd->ckd', prob_low, do_heads, preferred_element_type=j...]
    ppermute x0 -> x15, waiting for transfers between devices: none -> 71.1 us  [swapped(): lax.ppermute(value, axis, [(source, source ^ flip) for source in range(co...]
    all_to_all x3 -> x0, waiting for transfers between devices: 57.1 us -> none  [the longest x1 39.9 us: shards(): lax.all_to_all(dq_stack, 'head', split_axis=1, concat_axis=2, tiled=True)]
    another operation x13 -> x0, local copies, waits for them, and re-layouts: 53.9 us -> none  [the longest x1 16.3 us: shards(): jnp.stack([entry[0].reshape(tok_local, head_local * HEAD_SIZE) for entry...]
    unnamed x44 -> x60, local copies, waits for them, and re-layouts: 60 us -> 9.04 us
    slice x15 -> x0, local copies, waits for them, and re-layouts: 30 us -> none  [the longest x1 6.39 us: shards(): queries[layer_number].reshape(tok_local, head_local, HEAD_SIZE)]
    all_to_all x6 -> x0, local copies, waits for them, and re-layouts: 27 us -> none  [the longest x2 16.2 us: shards(): lax.all_to_all(dq_stack, 'head', split_axis=1, concat_axis=2, tiled=True)]
  transfers between devices with their start and end apart: 7 -> 23, of which waited for: 4 -> 7; matrix products, arithmetic and copies ran while one was open for 24% -> 1% of each run, Pallas kernels for 0% -> 73%
where the time goes in v1:
time: 654 us; the launch traced here: 653 us
  Pallas kernels  524 us (80%)
  waiting for transfers between devices  76.4 us (12%)
  starting transfers between devices  35.5 us (5%)
  local copies, waits for them, and re-layouts  11.6 us (2%)
    pallas_call x5, Pallas kernels, place_call(): pl.pallas_call(functools.partial(place_kernel, plan, owners, group, kv_lo...  390 us
    pallas_call x4, Pallas kernels, band_call(): pl.pallas_call(functools.partial(band_kernel, layer, kv_first, kv_count,...  125 us
    ppermute x15, waiting for transfers between devices, swapped(): lax.ppermute(value, axis, [(source, source ^ flip) for source in range(co...  71.1 us
    ppermute x15, starting transfers between devices, swapped(): lax.ppermute(value, axis, [(source, source ^ flip) for source in range(co...  18.7 us
    ppermute x8, starting transfers between devices, shifted(): lax.ppermute(value, axis, [(source, source + steps) for source in range(f...  16.8 us
  transfers between devices with their start and end apart: 23, of which 7 were waited for; matrix products, arithmetic and copies ran while one was open for 1% of the time, Pallas kernels for 73%

profile of v1, /device:TPU:24, one launch (start us, length us, event | category | flops | bytes accessed | tf_op | source)
XLA Modules:
  0.0 653.2 jit_solution(10743345306019575006)
XLA Ops:
  0.6 2.6 slice_bitcast_fusion.2
  10.3 2.0 collective-permute-start.5
  15.5 5.2 collective-permute-done.15.halo_ref
  22.6 31.4 %band.7 = (bf16[384,512]{1,0:T(8,128)(2,1)S(1)}, bf16[384,512]{1,0:T(8,128)(2,1)}, bf16[384,512]{1,0:T(8,128)(2,1)}, bf16[384,512]{1,0:T(8,128)(2,1)S(1)}, bf16[...) custom-call(s32[4]{0:T(128)S(1)} %pad_add_fusion.scal, bf16[2,1536,1024]{2,1,0:T(8,128)(2,1)} %q_ref.7, ...), custom_call_target="tpu_custom_call" | custom-call | flops 20132659200 | bytes 6291456 | tf_op jit(solution)/shard_map/band/pallas_call | solution.py:150
  59.8 31.8 %band.6 = (bf16[384,1024]{1,0:T(8,128)(2,1)S(1)}, bf16[384,1024]{1,0:T(8,128)(2,1)S(1)}, bf16[384,1024]{1,0:T(8,128)(2,1)}, bf16[384,1024]{1,0:T(8,128)(2,1)}, b...) custom-call(s32[4]{0:T(128)S(1)} %pad_add_fusion.scal, bf16[2,1536,1024]{2,1,0:T(8,128)(2,1)} %q_ref.7, ...), custom_call_target="tpu_custom_call" | custom-call | flops 20132659200 | bytes 6291456 | tf_op jit(solution)/shard_map/band/pallas_call | solution.py:150
  92.4 2.5 collective-permute-start.11
  94.9 30.9 %band.5 = (bf16[384,1024]{1,0:T(8,128)(2,1)S(1)}, bf16[384,1024]{1,0:T(8,128)(2,1)S(1)}, bf16[384,1024]{1,0:T(8,128)(2,1)S(1)}, bf16[384,1024]{1,0:T(8,128)(2,1)...) custom-call(s32[4]{0:T(128)S(1)} %pad_add_fusion.scal, bf16[2,1536,1024]{2,1,0:T(8,128)(2,1)} %q_ref.7, ...), custom_call_target="tpu_custom_call" | custom-call | flops 20132659200 | bytes 6291456 | tf_op jit(solution)/shard_map/band/pallas_call | solution.py:150
  127.7 2.2 collective-permute-start.6
  129.9 31.2 %band.4 = (bf16[384,1024]{1,0:T(8,128)(2,1)S(1)}, bf16[384,1024]{1,0:T(8,128)(2,1)S(1)}, bf16[384,1024]{1,0:T(8,128)(2,1)}, bf16[384,1024]{1,0:T(8,128)(2,1)}, b...) custom-call(s32[4]{0:T(128)S(1)} %pad_add_fusion.scal, bf16[2,1536,1024]{2,1,0:T(8,128)(2,1)} %q_ref.7, ...), custom_call_target="tpu_custom_call" | custom-call | flops 20132659200 | bytes 6291456 | tf_op jit(solution)/shard_map/band/pallas_call | solution.py:150
  161.1 2.4 collective-permute-start.1
  165.3 2.7 finish.7
  171.1 2.0 finish.6
  173.2 3.4 collective-permute-done.22.rest_3_
  179.2 2.1 finish.5
  183.0 9.5 %collective-permute-done.17.rest_1_ = bf16[384,1024]{1,0:T(8,128)(2,1)S(1)} collective-permute-done((bf16[384,1024]{1,0:T(8,128)(2,1)S(1)}, bf16[384,1024]{1,0:T(8,128)(2,1)S(1)}, u32[]{:S(2)}, u32[]{:S(2)}) %collective-permute-start.17) | collective-permute-done | bytes 786464 | tf_op jit(solution)/shard_map/ppermute | solution.py:36
  195.4 14.9 %collective-permute-done.19.rest_3_ = bf16[384,1024]{1,0:T(8,128)(2,1)S(1)} collective-permute-done((bf16[384,1024]{1,0:T(8,128)(2,1)}, bf16[384,1024]{1,0:T(8,128)(2,1)S(1)}, u32[]{:S(2)}, u32[]{:S(2)}) %collective-permute-start.19) | collective-permute-done | bytes 786464 | tf_op jit(solution)/shard_map/ppermute | solution.py:36
  210.8 15.4 %collective-permute-done.12.rest_1_ = bf16[384,1024]{1,0:T(8,128)(2,1)S(1)} collective-permute-done((bf16[384,1024]{1,0:T(8,128)(2,1)S(1)}, bf16[384,1024]{1,0:T(8,128)(2,1)S(1)}, u32[]{:S(2)}, u32[]{:S(2)}) %collective-permute-start.12) | collective-permute-done | bytes 786464 | tf_op jit(solution)/shard_map/ppermute | solution.py:36
  231.4 12.7 %collective-permute-done.14.rest_3_ = bf16[384,1024]{1,0:T(8,128)(2,1)S(1)} collective-permute-done((bf16[384,1024]{1,0:T(8,128)(2,1)S(1)}, bf16[384,1024]{1,0:T(8,128)(2,1)S(1)}, u32[]{:S(2)}, u32[]{:S(2)}) %collective-permute-start.14) | collective-permute-done | bytes 786464 | tf_op jit(solution)/shard_map/ppermute | solution.py:36
  244.6 15.4 %collective-permute-done.7.rest_1_ = bf16[384,1024]{1,0:T(8,128)(2,1)S(1)} collective-permute-done((bf16[384,1024]{1,0:T(8,128)(2,1)S(1)}, bf16[384,1024]{1,0:T(8,128)(2,1)S(1)}, u32[]{:S(2)}, u32[]{:S(2)}) %collective-permute-start.7) | collective-permute-done | bytes 786464 | tf_op jit(solution)/shard_map/ppermute | solution.py:36
  261.4 49.4 %place.5 = (bf16[2,384,4096]{2,1,0:T(8,128)(2,1)}, bf16[2,384,2048]{2,1,0:T(8,128)(2,1)}, bf16[2,384,2048]{2,1,0:T(8,128)(2,1)}) custom-call(s32[4]{0:T(128)} %copy-done.14, bf16[384,512]{1,0:T(8,128)(2,1)} %copy-done.13, bf16[384,512]{1,0:T(8,128)(2,1)} %collective-permute-done.20.rest_1_, bf16[384,512]{1,0:T(8,128)(2,1)} %collective-permute-done.21.rest_2_, ...), custom_call_target="tpu_custom_call" | custom-call | bytes 3145728 | tf_op jit(solution)/shard_map/place/pallas_call | solution.py:304
  310.9 97.2 %place.6 = (bf16[2,384,4096]{2,1,0:T(8,128)(2,1)}, bf16[2,384,2048]{2,1,0:T(8,128)(2,1)}, bf16[2,384,2048]{2,1,0:T(8,128)(2,1)}) custom-call(s32[4]{0:T(128)} %copy-done.14, bf16[384,1024]{1,0:T(8,128)(2,1)} %copy-done.2, bf16[384,1024]{1,0:T(8,128)(2,1)} %copy-done.18, ...), custom_call_target="tpu_custom_call", output_to_operand_aliasing={{0}: (5, {}), {1}: (6, {}), {2}: (7, {})} | custom-call | bytes 6291456 | tf_op jit(solution)/shard_map/place/pallas_call | solution.py:304
  408.1 97.2 %place.7 = (bf16[2,384,4096]{2,1,0:T(8,128)(2,1)}, bf16[2,384,2048]{2,1,0:T(8,128)(2,1)}, bf16[2,384,2048]{2,1,0:T(8,128)(2,1)}) custom-call(s32[4]{0:T(128)} %copy-done.14, bf16[384,1024]{1,0:T(8,128)(2,1)} %copy-done.1, bf16[384,1024]{1,0:T(8,128)(2,1)} %copy-done.20, ...), custom_call_target="tpu_custom_call", output_to_operand_aliasing={{0}: (5, {}), {1}: (6, {}), {2}: (7, {})} | custom-call | bytes 6291456 | tf_op jit(solution)/shard_map/place/pallas_call | solution.py:304
  505.3 97.2 %place.8 = (bf16[2,384,4096]{2,1,0:T(8,128)(2,1)}, bf16[2,384,2048]{2,1,0:T(8,128)(2,1)}, bf16[2,384,2048]{2,1,0:T(8,128)(2,1)}) custom-call(s32[4]{0:T(128)} %copy-done.14, bf16[384,1024]{1,0:T(8,128)(2,1)} %copy-done, bf16[384,1024]{1,0:T(8,128)(2,1)} %copy-done.22, ...), custom_call_target="tpu_custom_call", output_to_operand_aliasing={{0}: (5, {}), {1}: (6, {}), {2}: (7, {})} | custom-call | bytes 6291456 | tf_op jit(solution)/shard_map/place/pallas_call | solution.py:304
  603.5 49.5 %place.9 = (bf16[2,384,4096]{2,1,0:T(8,128)(2,1)}, bf16[2,384,2048]{2,1,0:T(8,128)(2,1)}, bf16[2,384,2048]{2,1,0:T(8,128)(2,1)}) custom-call(s32[4]{0:T(128)} %copy-done.14, bf16[384,512]{1,0:T(8,128)(2,1)} %copy-done.12, bf16[384,512]{1,0:T(8,128)(2,1)} %copy-done.25, ...), custom_call_target="tpu_custom_call", output_to_operand_aliasing={{0}: (5, {}), {1}: (6, {}), {2}: (7, {})} | custom-call | bytes 3145728 | tf_op jit(solution)/shard_map/place/pallas_call | solution.py:304
  (101 shorter events, 41.2 us)
Async XLA Ops:
  4.3 16.4 %collective-permute-start.15 = (bf16[1024,512]{1,0:T(8,128)(2,1)}, bf16[1024,512]{1,0:T(8,128)(2,1)}, u32[]{:S(2)}, u32[]{:S(2)}) collective-permute-start(bf16[1024,512]{1,0:T(8,128)(2,1)} %pad_maximum_fusion.3), channel_id=1, source_target_pairs={{0,4},{4,8},{8,12},{12,16},{16,20},{20,24},{24,28},{1,5},{5,9},{9,... | collective-permute-start | bytes 3145736 | tf_op jit(solution)/shard_map/ppermute | solution.py:31
  7.3 50.5 %collective-permute-start.10 = (bf16[1024,512]{1,0:T(8,128)(2,1)}, bf16[1024,512]{1,0:T(8,128)(2,1)}, u32[]{:S(2)}, u32[]{:S(2)}) collective-permute-start(bf16[1024,512]{1,0:T(8,128)(2,1)} %pad_maximum_fusion.2), channel_id=1, source_target_pairs={{0,4},{4,8},{8,12},{12,16},{16,20},{20,24},{24,28},{1,5},{5,9},{9,... | collective-permute-start | bytes 3145736 | tf_op jit(solution)/shard_map/ppermute | solution.py:31
  10.3 82.1 %collective-permute-start.5 = (bf16[1024,512]{1,0:T(8,128)(2,1)}, bf16[1024,512]{1,0:T(8,128)(2,1)}, u32[]{:S(2)}, u32[]{:S(2)}) collective-permute-start(bf16[1024,512]{1,0:T(8,128)(2,1)} %pad_maximum_fusion.1), channel_id=1, source_target_pairs={{0,4},{4,8},{8,12},{12,16},{16,20},{20,24},{24,28},{1,5},{5,9},{9,... | collective-permute-start | bytes 3145736 | tf_op jit(solution)/shard_map/ppermute | solution.py:31
  13.5 114.2 %collective-permute-start = (bf16[1024,512]{1,0:T(8,128)(2,1)}, bf16[1024,512]{1,0:T(8,128)(2,1)}, u32[]{:S(2)}, u32[]{:S(2)}) collective-permute-start(bf16[1024,512]{1,0:T(8,128)(2,1)} %pad_maximum_fusion), channel_id=1, source_target_pairs={{0,4},{4,8},{8,12},{12,16},{16,20},{20,24},{24,28},{1,5},{5,9},{9,... | collective-permute-start | bytes 3145736 | tf_op jit(solution)/shard_map/ppermute | solution.py:31
  15.5 212.2 %copy-start.14 = (s32[4]{0:T(128)}, s32[4]{0:T(128)S(1)}, u32[]{:S(2)}) copy-start(s32[4]{0:T(128)S(1)} %pad_add_fusion.scal) | copy-start | bytes 52
  54.8 106.3 %collective-permute-start.20 = (bf16[384,512]{1,0:T(8,128)(2,1)}, bf16[384,512]{1,0:T(8,128)(2,1)}, u32[]{:S(2)}, u32[]{:S(2)}) collective-permute-start(bf16[384,512]{1,0:T(8,128)(2,1)} %get-tuple-element.92), channel_id=1, source_target_pairs={{0,1},{1,0},{2,3},{3,2},{4,5},{5,4},{6,7},{7,6},{8,9},{9,8},{10,11... | collective-permute-start | bytes 1179656 | tf_op jit(solution)/shard_map/ppermute | solution.py:36
  56.3 111.7 %collective-permute-start.21 = (bf16[384,512]{1,0:T(8,128)(2,1)}, bf16[384,512]{1,0:T(8,128)(2,1)}, u32[]{:S(2)}, u32[]{:S(2)}) collective-permute-start(bf16[384,512]{1,0:T(8,128)(2,1)} %get-tuple-element.93), channel_id=1, source_target_pairs={{0,2},{1,3},{2,0},{3,1},{4,6},{5,7},{6,4},{7,5},{8,10},{9,11},{10,... | collective-permute-start | bytes 1179656 | tf_op jit(solution)/shard_map/ppermute | solution.py:36
  57.8 105.7 %collective-permute-start.16 = (bf16[1024,512]{1,0:T(8,128)(2,1)}, bf16[1024,512]{1,0:T(8,128)(2,1)}, u32[]{:S(2)}, u32[]{:S(2)}) collective-permute-start(bf16[1024,512]{1,0:T(8,128)(2,1)} %get-tuple-element.82), channel_id=1, source_target_pairs={{4,0},{8,4},{12,8},{16,12},{20,16},{24,20},{28,24},{5,1},{9,5},{13... | collective-permute-start | bytes 3145736 | tf_op jit(solution)/shard_map/ppermute | solution.py:31
  92.4 77.1 %collective-permute-start.11 = (bf16[1024,512]{1,0:T(8,128)(2,1)}, bf16[1024,512]{1,0:T(8,128)(2,1)}, u32[]{:S(2)}, u32[]{:S(2)}) collective-permute-start(bf16[1024,512]{1,0:T(8,128)(2,1)} %get-tuple-element.72), channel_id=1, source_target_pairs={{4,0},{8,4},{12,8},{16,12},{20,16},{24,20},{28,24},{5,1},{9,5},{13... | collective-permute-start | bytes 3145736 | tf_op jit(solution)/shard_map/ppermute | solution.py:31
  127.7 50.1 %collective-permute-start.6 = (bf16[1024,512]{1,0:T(8,128)(2,1)}, bf16[1024,512]{1,0:T(8,128)(2,1)S(1)}, u32[]{:S(2)}, u32[]{:S(2)}) collective-permute-start(bf16[1024,512]{1,0:T(8,128)(2,1)} %get-tuple-element.62), channel_id=1, source_target_pairs={{4,0},{8,4},{12,8},{16,12},{20,16},{24,20},{28,24},{5,1},{9,5},{13... | collective-permute-start | bytes 3145736 | tf_op jit(solution)/shard_map/ppermute | solution.py:31
  161.1 20.3 %collective-permute-start.1 = (bf16[1024,512]{1,0:T(8,128)(2,1)S(1)}, bf16[1024,512]{1,0:T(8,128)(2,1)S(1)}, u32[]{:S(2)}, u32[]{:S(2)}) collective-permute-start(bf16[1024,512]{1,0:T(8,128)(2,1)S(1)} %get-tuple-element.56), channel_id=1, source_target_pairs={{4,0},{8,4},{12,8},{16,12},{20,16},{24,20},{28,24},{5,1},{9,5},{13... | collective-permute-start | bytes 3145736 | tf_op jit(solution)/shard_map/ppermute | solution.py:31
  163.6 13.0 %collective-permute-start.22 = (bf16[384,512]{1,0:T(8,128)(2,1)S(1)}, bf16[384,512]{1,0:T(8,128)(2,1)S(1)}, u32[]{:S(2)}, u32[]{:S(2)}) collective-permute-start(bf16[384,512]{1,0:T(8,128)(2,1)S(1)} %copy-done.16), channel_id=1, source_target_pairs={{0,3},{1,2},{2,1},{3,0},{4,7},{5,6},{6,5},{7,4},{8,11},{9,10},{10,... | collective-permute-start | bytes 1179656 | tf_op jit(solution)/shard_map/ppermute | solution.py:36
  168.0 24.4 %collective-permute-start.17 = (bf16[384,1024]{1,0:T(8,128)(2,1)S(1)}, bf16[384,1024]{1,0:T(8,128)(2,1)S(1)}, u32[]{:S(2)}, u32[]{:S(2)}) collective-permute-start(bf16[384,1024]{1,0:T(8,128)(2,1)S(1)} %get-tuple-element.88), channel_id=1, source_target_pairs={{0,1},{1,0},{2,3},{3,2},{4,5},{5,4},{6,7},{7,6},{8,9},{9,8},{10,11... | collective-permute-start | bytes 2359304 | tf_op jit(solution)/shard_map/ppermute | solution.py:36
  169.6 24.4 %collective-permute-start.18 = (bf16[384,1024]{1,0:T(8,128)(2,1)}, bf16[384,1024]{1,0:T(8,128)(2,1)S(1)}, u32[]{:S(2)}, u32[]{:S(2)}) collective-permute-start(bf16[384,1024]{1,0:T(8,128)(2,1)} %get-tuple-element.89), channel_id=1, source_target_pairs={{0,2},{1,3},{2,0},{3,1},{4,6},{5,7},{6,4},{7,5},{8,10},{9,11},{10,... | collective-permute-start | bytes 2359304 | tf_op jit(solution)/shard_map/ppermute | solution.py:36
  177.3 33.0 %collective-permute-start.19 = (bf16[384,1024]{1,0:T(8,128)(2,1)}, bf16[384,1024]{1,0:T(8,128)(2,1)S(1)}, u32[]{:S(2)}, u32[]{:S(2)}) collective-permute-start(bf16[384,1024]{1,0:T(8,128)(2,1)} %get-tuple-element.90), channel_id=1, source_target_pairs={{0,3},{1,2},{2,1},{3,0},{4,7},{5,6},{6,5},{7,4},{8,11},{9,10},{10,... | collective-permute-start | bytes 2359304 | tf_op jit(solution)/shard_map/ppermute | solution.py:36
  177.8 48.4 %collective-permute-start.12 = (bf16[384,1024]{1,0:T(8,128)(2,1)S(1)}, bf16[384,1024]{1,0:T(8,128)(2,1)S(1)}, u32[]{:S(2)}, u32[]{:S(2)}) collective-permute-start(bf16[384,1024]{1,0:T(8,128)(2,1)S(1)} %get-tuple-element.78), channel_id=1, source_target_pairs={{0,1},{1,0},{2,3},{3,2},{4,5},{5,4},{6,7},{7,6},{8,9},{9,8},{10,11... | collective-permute-start | bytes 2359304 | tf_op jit(solution)/shard_map/ppermute | solution.py:36
  181.4 48.5 %collective-permute-start.13 = (bf16[384,1024]{1,0:T(8,128)(2,1)S(1)}, bf16[384,1024]{1,0:T(8,128)(2,1)S(1)}, u32[]{:S(2)}, u32[]{:S(2)}) collective-permute-start(bf16[384,1024]{1,0:T(8,128)(2,1)S(1)} %get-tuple-element.79), channel_id=1, source_target_pairs={{0,2},{1,3},{2,0},{3,1},{4,6},{5,7},{6,4},{7,5},{8,10},{9,11},{10,... | collective-permute-start | bytes 2359304 | tf_op jit(solution)/shard_map/ppermute | solution.py:36
  192.4 51.6 %collective-permute-start.14 = (bf16[384,1024]{1,0:T(8,128)(2,1)S(1)}, bf16[384,1024]{1,0:T(8,128)(2,1)S(1)}, u32[]{:S(2)}, u32[]{:S(2)}) collective-permute-start(bf16[384,1024]{1,0:T(8,128)(2,1)S(1)} %get-tuple-element.80), channel_id=1, source_target_pairs={{0,3},{1,2},{2,1},{3,0},{4,7},{5,6},{6,5},{7,4},{8,11},{9,10},{10,... | collective-permute-start | bytes 2359304 | tf_op jit(solution)/shard_map/ppermute | solution.py:36
  193.9 66.0 %collective-permute-start.7 = (bf16[384,1024]{1,0:T(8,128)(2,1)S(1)}, bf16[384,1024]{1,0:T(8,128)(2,1)S(1)}, u32[]{:S(2)}, u32[]{:S(2)}) collective-permute-start(bf16[384,1024]{1,0:T(8,128)(2,1)S(1)} %get-tuple-element.68), channel_id=1, source_target_pairs={{0,1},{1,0},{2,3},{3,2},{4,5},{5,4},{6,7},{7,6},{8,9},{9,8},{10,11... | collective-permute-start | bytes 2359304 | tf_op jit(solution)/shard_map/ppermute | solution.py:36
  210.3 295.0 %collective-permute-start.8 = (bf16[384,1024]{1,0:T(8,128)(2,1)}, bf16[384,1024]{1,0:T(8,128)(2,1)}, u32[]{:S(2)}, u32[]{:S(2)}) collective-permute-start(bf16[384,1024]{1,0:T(8,128)(2,1)} %get-tuple-element.69), channel_id=1, source_target_pairs={{0,2},{1,3},{2,0},{3,1},{4,6},{5,7},{6,4},{7,5},{8,10},{9,11},{10,... | collective-permute-start | bytes 2359304 | tf_op jit(solution)/shard_map/ppermute | solution.py:36
  226.2 279.1 %collective-permute-start.9 = (bf16[384,1024]{1,0:T(8,128)(2,1)}, bf16[384,1024]{1,0:T(8,128)(2,1)}, u32[]{:S(2)}, u32[]{:S(2)}) collective-permute-start(bf16[384,1024]{1,0:T(8,128)(2,1)} %get-tuple-element.70), channel_id=1, source_target_pairs={{0,3},{1,2},{2,1},{3,0},{4,7},{5,6},{6,5},{7,4},{8,11},{9,10},{10,... | collective-permute-start | bytes 2359304 | tf_op jit(solution)/shard_map/ppermute | solution.py:36
  229.9 372.6 %collective-permute-start.2 = (bf16[384,512]{1,0:T(8,128)(2,1)S(1)}, bf16[384,512]{1,0:T(8,128)(2,1)S(1)}, u32[]{:S(2)}, u32[]{:S(2)}) collective-permute-start(bf16[384,512]{1,0:T(8,128)(2,1)S(1)} %get-tuple-element.58), channel_id=1, source_target_pairs={{0,1},{1,0},{2,3},{3,2},{4,5},{5,4},{6,7},{7,6},{8,9},{9,8},{10,11... | collective-permute-start | bytes 1179656 | tf_op jit(solution)/shard_map/ppermute | solution.py:36
  244.1 358.4 %collective-permute-start.3 = (bf16[384,512]{1,0:T(8,128)(2,1)S(1)}, bf16[384,512]{1,0:T(8,128)(2,1)S(1)}, u32[]{:S(2)}, u32[]{:S(2)}) collective-permute-start(bf16[384,512]{1,0:T(8,128)(2,1)S(1)} %get-tuple-element.59), channel_id=1, source_target_pairs={{0,2},{1,3},{2,0},{3,1},{4,6},{5,7},{6,4},{7,5},{8,10},{9,11},{10,... | collective-permute-start | bytes 1179656 | tf_op jit(solution)/shard_map/ppermute | solution.py:36
  259.9 342.6 %collective-permute-start.4 = (bf16[384,512]{1,0:T(8,128)(2,1)S(1)}, bf16[384,512]{1,0:T(8,128)(2,1)S(1)}, u32[]{:S(2)}, u32[]{:S(2)}) collective-permute-start(bf16[384,512]{1,0:T(8,128)(2,1)S(1)} %get-tuple-element.60), channel_id=1, source_target_pairs={{0,3},{1,2},{2,1},{3,0},{4,7},{5,6},{6,5},{7,4},{8,11},{9,10},{10,... | collective-permute-start | bytes 1179656 | tf_op jit(solution)/shard_map/ppermute | solution.py:36
  (29 other events, 517.3 us)

commit v2 on v1

--- a/solution.py
+++ b/solution.py
@@ -37,10 +37,10 @@
 
 
 def band_kernel(
-    layer, kv_first, kv_count, owners, scal, q_ref, do_ref, out_ref, lse_ref, k_ref, v_ref, halo_ref, *rest
+    layer, kv_first, kv_count, owners, scal, q_ref, do_ref, out_ref, lse_ref, k_ref, v_ref, halo_ref, after, *rest
 ):
     dq_bufs = rest[:owners]
-    back_ref, part_ref, kx, vx, kt, acc, dq_scr, sems = rest[owners:]
+    back_ref, part_ref, kx, vx, kt, acc, lse2_scr, delta_scr, dq_scr, sems = rest[owners:]
     tok_local = q_ref.shape[1]
     group = q_ref.shape[2] // HEAD_SIZE
     chunk = tok_local // owners
@@ -66,41 +66,50 @@
             [block[:, h * HEAD_SIZE : (h + 1) * HEAD_SIZE] for h in range(group)], 0
         )
 
+    ones = jnp.ones((8, HEAD_SIZE), jnp.bfloat16)
+    head = (kv_first + step) * group
+    for block in range(tok_local // TILE):
+        start = block * TILE
+        columns = slice(block * wide, (block + 1) * wide)
+        prod = stacked(do_ref, start).astype(jnp.float32) * stacked(out_ref, start).astype(jnp.float32)
+        high = prod.astype(jnp.bfloat16)
+        low = (prod - high.astype(jnp.float32)).astype(jnp.bfloat16)
+        delta_scr[:, columns] = dot(ones, high, NT) + dot(ones, low, NT)
+        for h in range(group):
+            lse2_scr[0:1, block * wide + h * TILE : block * wide + (h + 1) * TILE] = (
+                lse_ref[0, pl.ds(head + h, 1), start : start + TILE] * LOG2E
+            )
+
     def one_block(block, carry):
         start = pl.multiple_of(block * TILE, TILE)
+        columns = pl.ds(pl.multiple_of(block * wide, wide), wide)
         q2 = stacked(q_ref, start)
         do2 = stacked(do_ref, start)
-        prod = do2.astype(jnp.float32) * stacked(out_ref, start).astype(jnp.float32)
-        high = prod.astype(jnp.bfloat16)
-        low = (prod - high.astype(jnp.float32)).astype(jnp.bfloat16)
-        ones = jnp.ones((8, HEAD_SIZE), jnp.bfloat16)
-        delta = (dot(ones, high, NT) + dot(ones, low, NT))[0:1]
-        head = (kv_first + step) * group
-        lse = jnp.concatenate(
-            [lse_ref[0, pl.ds(head + h, 1), pl.ds(start, TILE)] for h in range(group)], 1
-        )
-        lse2 = lse * LOG2E
-        dq_t = jnp.zeros((HEAD_SIZE, wide), jnp.float32)
+        delta = delta_scr[0:1, columns]
+        lse2 = lse2_scr[0:1, columns]
         tiles = WINDOW_LENGTH // TILE + 1
+        span = pl.ds(start, tiles * TILE)
+        scores = dot(kx[span, :], q2, NT)
+        grad_prob = dot(vx[span, :], do2, NT)
+        prob_low = []
+        score_low = []
         for tile in range(tiles):
-            begin = pl.multiple_of(start + tile * TILE, TILE)
-            span = pl.ds(begin, TILE)
-            scores = dot(kx[span, :], q2, NT)
-            prob = jnp.exp2(scores * (SCALE * LOG2E) - lse2)
+            part = slice(tile * TILE, (tile + 1) * TILE)
+            prob = jnp.exp2(scores[part] * (SCALE * LOG2E) - lse2)
             if tile == tiles - 1:
                 seen = rows <= lanes
             else:
                 bound = WINDOW_LENGTH - win - tile * TILE
-                outside = jnp.logical_and(first_shard == 1, begin < WINDOW_LENGTH)
+                outside = jnp.logical_and(first_shard == 1, start + tile * TILE < WINDOW_LENGTH)
                 seen = rows > lanes + jnp.where(outside, FAR, bound)
             prob = jnp.where(seen, prob, 0.0)
-            grad_prob = dot(vx[span, :], do2, NT)
-            grad_score = prob * (grad_prob - delta)
-            prob_low = prob.astype(jnp.bfloat16)
-            score_low = grad_score.astype(jnp.bfloat16)
-            acc[span, HEAD_SIZE:] += dot(prob_low, do2)
-            acc[span, :HEAD_SIZE] += dot(score_low, q2)
-            dq_t += dot(kt[:, span], score_low)
+            prob_low.append(prob.astype(jnp.bfloat16))
+            score_low.append((prob * (grad_prob[part] - delta)).astype(jnp.bfloat16))
+        prob_low = jnp.concatenate(prob_low, 0)
+        score_low = jnp.concatenate(score_low, 0)
+        acc[span, HEAD_SIZE:] += dot(prob_low, do2)
+        acc[span, :HEAD_SIZE] += dot(score_low, q2)
+        dq_t = dot(kt[:, span], score_low)
         dq = (dq_t.T * SCALE).astype(jnp.bfloat16)
         for h in range(group):
             dq_scr[step, pl.ds(start, TILE), h * HEAD_SIZE : (h + 1) * HEAD_SIZE] = dq[
@@ -138,7 +147,7 @@
                 copy.wait()
 
 
-def band_call(piece, extra, owners, scal, queries, grad_out, attn_out, log_norm, keys, values, halo):
+def band_call(piece, extra, owners, scal, queries, grad_out, attn_out, log_norm, keys, values, halo, column, after):
     layer, kv_first, kv_count = piece
     tok_local = queries.shape[1]
     group = queries.shape[2] // keys.shape[2]
@@ -158,7 +167,8 @@
             pl.BlockSpec((1,) + log_norm.shape[1:], lambda g: (layer, 0, 0)),
             kv_spec,
             kv_spec,
-            pl.BlockSpec((WINDOW_LENGTH, 2 * HEAD_SIZE), lambda g: (0, g)),
+            pl.BlockSpec((WINDOW_LENGTH, 2 * HEAD_SIZE), lambda g: (0, column + g)),
+            pl.BlockSpec(memory_space=pl.ANY),
         ],
         out_specs=[pl.BlockSpec(memory_space=pl.ANY)] * owners
         + [
@@ -178,6 +188,8 @@
             pltpu.VMEM((span, HEAD_SIZE), jnp.bfloat16),
             pltpu.VMEM((HEAD_SIZE, span), jnp.bfloat16),
             pltpu.VMEM((span, 2 * HEAD_SIZE), jnp.float32),
+            pltpu.VMEM((8, tok_local * group), jnp.float32),
+            pltpu.VMEM((8, tok_local * group), jnp.float32),
             pltpu.VMEM((kv_count, tok_local, group * HEAD_SIZE), jnp.bfloat16),
             pltpu.SemaphoreType.DMA((kv_count, owners)),
         ],
@@ -188,7 +200,7 @@
             transcendentals=pairs,
         ),
         name="band",
-    )(scal, queries, grad_out, attn_out, log_norm, keys, values, halo)
+    )(scal, queries, grad_out, attn_out, log_norm, keys, values, halo, after)
     return outs[:owners], outs[owners], outs[owners + 1]
 
 
@@ -266,10 +278,17 @@
 def place_kernel(plan, owners, group, kv_local, aliased, scal, *rest):
     blocks = rest[:owners]
     outs = rest[owners + (3 if aliased else 0) :][:3]
-    sems = rest[-1]
+    scr, in_sems, out_sems = rest[-3:]
     me = scal[0]
-    copies = []
+    loads = [
+        pltpu.make_async_copy(blocks[flip], scr.at[flip], in_sems.at[flip])
+        for flip in range(owners)
+    ]
+    for load in loads:
+        load.start()
+    stores = []
     for flip in range(owners):
+        loads[flip].wait()
         source = jnp.bitwise_xor(me, flip)
         column = 0
         for which, (layer, kv_first, kv_count) in plan:
@@ -277,18 +296,16 @@
             home = kv_local * group if which == 0 else kv_local
             first = kv_first * group if which == 0 else kv_first
             place = pl.multiple_of((source * home + first) * HEAD_SIZE, HEAD_SIZE)
-            copies.append(
-                pltpu.make_async_copy(
-                    blocks[flip].at[:, pl.ds(column, heads * HEAD_SIZE)],
-                    outs[which].at[layer, :, pl.ds(place, heads * HEAD_SIZE)],
-                    sems.at[len(copies)],
-                )
+            store = pltpu.make_async_copy(
+                scr.at[flip, :, pl.ds(column, heads * HEAD_SIZE)],
+                outs[which].at[layer, :, pl.ds(place, heads * HEAD_SIZE)],
+                out_sems.at[len(stores)],
             )
+            store.start()
+            stores.append(store)
             column += heads * HEAD_SIZE
-    for copy in copies:
-        copy.start()
-    for copy in copies:
-        copy.wait()
+    for store in stores:
+        store.wait()
 
 
 def place_call(plan, owners, group, kv_local, scal, blocks, outs):
@@ -308,7 +325,12 @@
         out_specs=[any_spec] * 3,
         out_shape=shapes,
         input_output_aliases={1 + owners + i: i for i in range(3)} if aliased else {},
-        scratch_shapes=[pltpu.SemaphoreType.DMA((owners * len(plan),))],
+        scratch_shapes=[
+            pltpu.VMEM((owners, chunk, width), jnp.bfloat16),
+            pltpu.SemaphoreType.DMA((owners,)),
+            pltpu.SemaphoreType.DMA((owners * len(plan),)),
+        ],
+        compiler_params=pltpu.CompilerParams(vmem_limit_bytes=16 * 1024 * 1024),
         cost_estimate=pl.CostEstimate(
             flops=0, bytes_accessed=owners * chunk * width * 4, transcendentals=0
         ),
@@ -335,14 +357,18 @@
         for kv_first in range(0, kv_local, each)
     ]
 
-    halos = []
-    for layer, kv_first, kv_count in pieces:
+    def halo_of(some):
         parts = []
-        for kv in range(kv_first, kv_first + kv_count):
-            columns = slice(kv * HEAD_SIZE, (kv + 1) * HEAD_SIZE)
-            parts.append(layer_keys_input[layer, tok_local - WINDOW_LENGTH :, columns])
-            parts.append(layer_values_input[layer, tok_local - WINDOW_LENGTH :, columns])
-        halos.append(shifted(jnp.concatenate(parts, 1), "ctx", 1))
+        for layer, kv_first, kv_count in some:
+            for kv in range(kv_first, kv_first + kv_count):
+                columns = slice(kv * HEAD_SIZE, (kv + 1) * HEAD_SIZE)
+                parts.append(layer_keys_input[layer, tok_local - WINDOW_LENGTH :, columns])
+                parts.append(layer_values_input[layer, tok_local - WINDOW_LENGTH :, columns])
+        return shifted(jnp.concatenate(parts, 1), "ctx", 1)
+
+    first_halo = halo_of(pieces[:1])
+    other_halo = halo_of(pieces[1:])
+    halos = [(first_halo, 0)] + [(other_halo, index * each) for index in range(len(pieces) - 1)]
 
     outs = None
     waiting = None
@@ -351,7 +377,8 @@
         blocks = [bufs[0]] + [swapped(bufs[flip], "head", flip) for flip in range(1, owners)]
         return place_call(plan, owners, group, kv_local, scal, blocks, outs)
 
-    for piece, halo in zip(pieces, halos):
+    after = scal
+    for piece, (halo, column) in zip(pieces, halos):
         kv_count = piece[2]
         extra = 0 if waiting is None else 2 * waiting[0][2]
         bufs, back, part = band_call(
@@ -366,7 +393,10 @@
             layer_keys_input,
             layer_values_input,
             halo,
+            column,
+            after,
         )
+        after = part
         back = shifted(back, "ctx", -1)
         plan = [(0, piece)]
         if waiting is not None:
@@ -374,6 +404,7 @@
             bufs = finish_call(
                 old[2], owners, kv_count * group * HEAD_SIZE, scal, old_part, old_back, bufs
             )
+            after = bufs[0]
             plan += [(1, old), (2, old)]
         outs = send(plan, bufs, outs)
         waiting = (piece, part, back)

time: 654 us -> 307 us (0.47)
  Pallas kernels: 524 us -> 140 us
  waiting for transfers between devices: 76.4 us -> 109 us
  local copies, waits for them, and re-layouts: 11.6 us -> 23.8 us
    pallas_call x5, Pallas kernels: 390 us -> 12.7 us  [place_call(): pl.pallas_call(functools.partial(place_kernel, plan, owners, group, kv_lo...]
    ppermute x8 -> x6, waiting for transfers between devices: 5.25 us -> 44 us  [shifted(): lax.ppermute(value, axis, [(source, source + steps) for source in range(f...]
    unnamed x60 -> x35, local copies, waits for them, and re-layouts: 9.04 us -> 21 us
    ppermute x8 -> x6, starting transfers between devices: 16.8 us -> 12.2 us  [shifted(): lax.ppermute(value, axis, [(source, source + steps) for source in range(f...]
  transfers between devices with their start and end apart: 23 -> 21, of which waited for: 7 -> 5; matrix products, arithmetic and copies ran while one was open for 1% -> 1% of each run, Pallas kernels for 73% -> 45%
where the time goes in v2:
time: 307 us; the launch traced here: 306 us
  Pallas kernels  140 us (46%)
  waiting for transfers between devices  109 us (36%)
  starting transfers between devices  31 us (10%)
  local copies, waits for them, and re-layouts  23.8 us (8%)
    pallas_call x4, Pallas kernels, band_call(): pl.pallas_call(functools.partial(band_kernel, layer, kv_first, kv_count,...  120 us
    ppermute x15, waiting for transfers between devices, swapped(): lax.ppermute(value, axis, [(source, source ^ flip) for source in range(co...  65.2 us
    ppermute x6, waiting for transfers between devices, shifted(): lax.ppermute(value, axis, [(source, source + steps) for source in range(f...  44 us
    unnamed x35, local copies, waits for them, and re-layouts  21 us
    ppermute x15, starting transfers between devices, swapped(): lax.ppermute(value, axis, [(source, source ^ flip) for source in range(co...  18.9 us
    pallas_call x5, Pallas kernels, place_call(): pl.pallas_call(functools.partial(place_kernel, plan, owners, group, kv_lo...  12.7 us
    ppermute x6, starting transfers between devices, shifted(): lax.ppermute(value, axis, [(source, source + steps) for source in range(f...  12.2 us
    pallas_call x4, Pallas kernels, finish_call(): pl.pallas_call(functools.partial(finish_kernel, kv_count, owners, column,...  7.12 us
  transfers between devices with their start and end apart: 21, of which 5 were waited for; matrix products, arithmetic and copies ran while one was open for 1% of the time, Pallas kernels for 45%

profile of v2, /device:TPU:24, one launch (start us, length us, event | category | flops | bytes accessed | tf_op | source)
XLA Modules:
  0.0 306.4 jit_solution(4642760995776862941)
XLA Ops:
  19.0 1.9 collective-permute-start
  23.1 1.9 collective-permute-start.1
  25.1 44.0 %collective-permute-done.1.halo_ref = bf16[1024,512]{1,0:T(8,128)(2,1)} collective-permute-done((bf16[1024,512]{1,0:T(8,128)(2,1)}, bf16[1024,512]{1,0:T(8,128)(2,1)}, u32[]{:S(2)}, u32[]{:S(2)}) %collective-permute-start.1) | collective-permute-done | bytes 1048608 | tf_op jit(solution)/shard_map/ppermute | solution.py:31
  69.1 1.9 copy-done.3
  71.0 30.0 %band.4 = (bf16[384,512]{1,0:T(8,128)(2,1)S(1)}, bf16[384,512]{1,0:T(8,128)(2,1)S(1)}, bf16[384,512]{1,0:T(8,128)(2,1)S(1)}, bf16[384,512]{1,0:T(8,128)(2,1)}, b...) custom-call(s32[4]{0:T(128)S(1)} %pad_add_fusion.scal.after, bf16[2,1536,1024]{2,1,0:T(8,128)(2,1)} %q_ref.7, ...), custom_call_target="tpu_custom_call" | custom-call | flops 20132659200 | bytes 6291456 | tf_op jit(solution)/shard_map/band/pallas_call | solution.py:159
  102.6 1.9 collective-permute-start.3
  108.1 30.2 %band.5 = (bf16[384,1024]{1,0:T(8,128)(2,1)S(1)}, bf16[384,1024]{1,0:T(8,128)(2,1)S(1)}, bf16[384,1024]{1,0:T(8,128)(2,1)}, bf16[384,1024]{1,0:T(8,128)(2,1)}, b...) custom-call(s32[4]{0:T(128)S(1)} %pad_add_fusion.scal.after, bf16[2,1536,1024]{2,1,0:T(8,128)(2,1)} %q_ref.7, ...), custom_call_target="tpu_custom_call" | custom-call | flops 20132659200 | bytes 6291456 | tf_op jit(solution)/shard_map/band/pallas_call | solution.py:159
  138.4 2.1 finish.4
  142.1 2.1 collective-permute-start.2
  144.1 30.6 %band.6 = (bf16[384,1024]{1,0:T(8,128)(2,1)S(1)}, bf16[384,1024]{1,0:T(8,128)(2,1)}, bf16[384,1024]{1,0:T(8,128)(2,1)}, bf16[384,1024]{1,0:T(8,128)(2,1)}, bf16[...) custom-call(s32[4]{0:T(128)S(1)} %pad_add_fusion.scal.after, bf16[2,1536,1024]{2,1,0:T(8,128)(2,1)} %q_ref.7, ...), custom_call_target="tpu_custom_call" | custom-call | flops 20132659200 | bytes 6291456 | tf_op jit(solution)/shard_map/band/pallas_call | solution.py:159
  176.4 2.0 finish.5
  179.0 1.9 collective-permute-start.8
  180.9 29.5 %band.7 = (bf16[384,1024]{1,0:T(8,128)(2,1)S(1)}, bf16[384,1024]{1,0:T(8,128)(2,1)S(1)}, bf16[384,1024]{1,0:T(8,128)(2,1)S(1)}, bf16[384,1024]{1,0:T(8,128)(2,1)...) custom-call(s32[4]{0:T(128)S(1)} %pad_add_fusion.scal.after, bf16[2,1536,1024]{2,1,0:T(8,128)(2,1)} %q_ref.7, ...), custom_call_target="tpu_custom_call" | custom-call | flops 20132659200 | bytes 6291456 | tf_op jit(solution)/shard_map/band/pallas_call | solution.py:159
  211.2 2.4 collective-permute-start.4
  220.4 13.9 %collective-permute-done.12.rest_1_ = bf16[384,1024]{1,0:T(8,128)(2,1)S(1)} collective-permute-done((bf16[384,1024]{1,0:T(8,128)(2,1)}, bf16[384,1024]{1,0:T(8,128)(2,1)S(1)}, u32[]{:S(2)}, u32[]{:S(2)}) %collective-permute-start.12) | collective-permute-done | bytes 786464 | tf_op jit(solution)/shard_map/ppermute | solution.py:36
  234.3 2.4 collective-permute-start.11
  238.7 32.5 %collective-permute-done.13.rest_2_ = bf16[384,1024]{1,0:T(8,128)(2,1)S(1)} collective-permute-done((bf16[384,1024]{1,0:T(8,128)(2,1)}, bf16[384,1024]{1,0:T(8,128)(2,1)S(1)}, u32[]{:S(2)}, u32[]{:S(2)}) %collective-permute-start.13) | collective-permute-done | bytes 786464 | tf_op jit(solution)/shard_map/ppermute | solution.py:36
  273.3 14.8 %collective-permute-done.10.rest_2_ = bf16[384,1024]{1,0:T(8,128)(2,1)S(1)} collective-permute-done((bf16[384,1024]{1,0:T(8,128)(2,1)S(1)}, bf16[384,1024]{1,0:T(8,128)(2,1)S(1)}, u32[]{:S(2)}, u32[]{:S(2)}) %collective-permute-start.10) | collective-permute-done | bytes 786464 | tf_op jit(solution)/shard_map/ppermute | solution.py:36
  289.6 2.5 place.5
  292.1 2.5 place.6
  294.6 2.5 place.7
  297.2 2.5 place.8
  299.7 3.9 %collective-permute-done.6.rest_2_ = bf16[384,512]{1,0:T(8,128)(2,1)S(1)} collective-permute-done((bf16[384,512]{1,0:T(8,128)(2,1)S(1)}, bf16[384,512]{1,0:T(8,128)(2,1)S(1)}, u32[]{:S(2)}, u32[]{:S(2)}) %collective-permute-start.6) | collective-permute-done | bytes 393248 | tf_op jit(solution)/shard_map/ppermute | solution.py:36
  303.7 2.5 place.9
  (70 shorter events, 42.5 us)
Async XLA Ops:
  14.2 54.9 %copy-start.8 = (f32[2,8,1536]{2,1,0:T(8,128)S(1)}, f32[2,8,1536]{2,1,0:T(8,128)}, u32[]{:S(2)}) copy-start(f32[2,8,1536]{2,1,0:T(8,128)} %lse_ref.7) | copy-start | bytes 294916
  19.0 89.1 %collective-permute-start = (bf16[1024,1536]{1,0:T(8,128)(2,1)}, bf16[1024,1536]{1,0:T(8,128)(2,1)}, u32[]{:S(2)}, u32[]{:S(2)}) collective-permute-start(bf16[1024,1536]{1,0:T(8,128)(2,1)} %bitcast_dynamic-update-slice_fusion), channel_id=1, source_target_pairs={{0,4},{4,8},{8,12},{12,16},{16,20},{20,24},{24,28},{1,5},{5,9},{9,... | collective-permute-start | bytes 9437192 | tf_op jit(solution)/shard_map/ppermute | solution.py:31
  23.1 46.0 %collective-permute-start.1 = (bf16[1024,512]{1,0:T(8,128)(2,1)}, bf16[1024,512]{1,0:T(8,128)(2,1)}, u32[]{:S(2)}, u32[]{:S(2)}) collective-permute-start(bf16[1024,512]{1,0:T(8,128)(2,1)} %pad_maximum_fusion), channel_id=1, source_target_pairs={{0,4},{4,8},{8,12},{12,16},{16,20},{20,24},{24,28},{1,5},{5,9},{9,... | collective-permute-start | bytes 3145736 | tf_op jit(solution)/shard_map/ppermute | solution.py:31
  102.6 35.7 %collective-permute-start.3 = (bf16[1024,512]{1,0:T(8,128)(2,1)S(1)}, bf16[1024,512]{1,0:T(8,128)(2,1)S(1)}, u32[]{:S(2)}, u32[]{:S(2)}) collective-permute-start(bf16[1024,512]{1,0:T(8,128)(2,1)S(1)} %get-tuple-element.58), channel_id=1, source_target_pairs={{4,0},{8,4},{12,8},{16,12},{20,16},{24,20},{28,24},{5,1},{9,5},{13... | collective-permute-start | bytes 3145736 | tf_op jit(solution)/shard_map/ppermute | solution.py:31
  104.5 73.9 %collective-permute-start.18 = (bf16[384,512]{1,0:T(8,128)(2,1)S(1)}, bf16[384,512]{1,0:T(8,128)(2,1)S(1)}, u32[]{:S(2)}, u32[]{:S(2)}) collective-permute-start(bf16[384,512]{1,0:T(8,128)(2,1)S(1)} %get-tuple-element.92), channel_id=1, source_target_pairs={{0,1},{1,0},{2,3},{3,2},{4,5},{5,4},{6,7},{7,6},{8,9},{9,8},{10,11... | collective-permute-start | bytes 1179656 | tf_op jit(solution)/shard_map/ppermute | solution.py:36
  106.1 72.9 %collective-permute-start.19 = (bf16[384,512]{1,0:T(8,128)(2,1)S(1)}, bf16[384,512]{1,0:T(8,128)(2,1)S(1)}, u32[]{:S(2)}, u32[]{:S(2)}) collective-permute-start(bf16[384,512]{1,0:T(8,128)(2,1)S(1)} %get-tuple-element.93), channel_id=1, source_target_pairs={{0,2},{1,3},{2,0},{3,1},{4,6},{5,7},{6,4},{7,5},{8,10},{9,11},{10,... | collective-permute-start | bytes 1179656 | tf_op jit(solution)/shard_map/ppermute | solution.py:36
  107.6 102.8 %collective-permute-start.20 = (bf16[384,512]{1,0:T(8,128)(2,1)}, bf16[384,512]{1,0:T(8,128)(2,1)S(1)}, u32[]{:S(2)}, u32[]{:S(2)}) collective-permute-start(bf16[384,512]{1,0:T(8,128)(2,1)} %get-tuple-element.94), channel_id=1, source_target_pairs={{0,3},{1,2},{2,1},{3,0},{4,7},{5,6},{6,5},{7,4},{8,11},{9,10},{10,... | collective-permute-start | bytes 1179656 | tf_op jit(solution)/shard_map/ppermute | solution.py:36
  140.5 76.3 %collective-permute-start.15 = (bf16[384,1024]{1,0:T(8,128)(2,1)S(1)}, bf16[384,1024]{1,0:T(8,128)(2,1)S(1)}, u32[]{:S(2)}, u32[]{:S(2)}) collective-permute-start(bf16[384,1024]{1,0:T(8,128)(2,1)S(1)} %get-tuple-element.88), channel_id=1, source_target_pairs={{0,1},{1,0},{2,3},{3,2},{4,5},{5,4},{6,7},{7,6},{8,9},{9,8},{10,11... | collective-permute-start | bytes 2359304 | tf_op jit(solution)/shard_map/ppermute | solution.py:36
  142.1 32.7 %collective-permute-start.2 = (bf16[1024,512]{1,0:T(8,128)(2,1)S(1)}, bf16[1024,512]{1,0:T(8,128)(2,1)S(1)}, u32[]{:S(2)}, u32[]{:S(2)}) collective-permute-start(bf16[1024,512]{1,0:T(8,128)(2,1)S(1)} %get-tuple-element.57), channel_id=1, source_target_pairs={{4,0},{8,4},{12,8},{16,12},{20,16},{24,20},{28,24},{5,1},{9,5},{13... | collective-permute-start | bytes 3145736 | tf_op jit(solution)/shard_map/ppermute | solution.py:31
  174.8 43.6 %collective-permute-start.16 = (bf16[384,1024]{1,0:T(8,128)(2,1)}, bf16[384,1024]{1,0:T(8,128)(2,1)S(1)}, u32[]{:S(2)}, u32[]{:S(2)}) collective-permute-start(bf16[384,1024]{1,0:T(8,128)(2,1)} %get-tuple-element.89), channel_id=1, source_target_pairs={{0,2},{1,3},{2,0},{3,1},{4,6},{5,7},{6,4},{7,5},{8,10},{9,11},{10,... | collective-permute-start | bytes 2359304 | tf_op jit(solution)/shard_map/ppermute | solution.py:36
  178.4 40.4 %collective-permute-start.17 = (bf16[384,1024]{1,0:T(8,128)(2,1)}, bf16[384,1024]{1,0:T(8,128)(2,1)S(1)}, u32[]{:S(2)}, u32[]{:S(2)}) collective-permute-start(bf16[384,1024]{1,0:T(8,128)(2,1)} %get-tuple-element.90), channel_id=1, source_target_pairs={{0,3},{1,2},{2,1},{3,0},{4,7},{5,6},{6,5},{7,4},{8,11},{9,10},{10,... | collective-permute-start | bytes 2359304 | tf_op jit(solution)/shard_map/ppermute | solution.py:36
  179.0 34.6 %collective-permute-start.8 = (bf16[1024,512]{1,0:T(8,128)(2,1)}, bf16[1024,512]{1,0:T(8,128)(2,1)S(1)}, u32[]{:S(2)}, u32[]{:S(2)}) collective-permute-start(bf16[1024,512]{1,0:T(8,128)(2,1)} %get-tuple-element.76), channel_id=1, source_target_pairs={{4,0},{8,4},{12,8},{16,12},{20,16},{24,20},{28,24},{5,1},{9,5},{13... | collective-permute-start | bytes 3145736 | tf_op jit(solution)/shard_map/ppermute | solution.py:31
  211.2 25.6 %collective-permute-start.4 = (bf16[1024,512]{1,0:T(8,128)(2,1)S(1)}, bf16[1024,512]{1,0:T(8,128)(2,1)S(1)}, u32[]{:S(2)}, u32[]{:S(2)}) collective-permute-start(bf16[1024,512]{1,0:T(8,128)(2,1)S(1)} %get-tuple-element.70), channel_id=1, source_target_pairs={{4,0},{8,4},{12,8},{16,12},{20,16},{24,20},{28,24},{5,1},{9,5},{13... | collective-permute-start | bytes 3145736 | tf_op jit(solution)/shard_map/ppermute | solution.py:31
  213.6 20.7 %collective-permute-start.12 = (bf16[384,1024]{1,0:T(8,128)(2,1)}, bf16[384,1024]{1,0:T(8,128)(2,1)S(1)}, u32[]{:S(2)}, u32[]{:S(2)}) collective-permute-start(bf16[384,1024]{1,0:T(8,128)(2,1)} %get-tuple-element.85), channel_id=1, source_target_pairs={{0,1},{1,0},{2,3},{3,2},{4,5},{5,4},{6,7},{7,6},{8,9},{9,8},{10,11... | collective-permute-start | bytes 2359304 | tf_op jit(solution)/shard_map/ppermute | solution.py:36
  216.8 72.8 %copy-start.5 = (bf16[384,512]{1,0:T(8,128)(2,1)S(1)}, bf16[384,512]{1,0:T(8,128)(2,1)}, u32[]{:S(2)}) copy-start(bf16[384,512]{1,0:T(8,128)(2,1)} %copy-done.4) | copy-start | bytes 1179652
  216.8 72.8 %copy-start.7 = (bf16[384,512]{1,0:T(8,128)(2,1)S(1)}, bf16[384,512]{1,0:T(8,128)(2,1)}, u32[]{:S(2)}) copy-start(bf16[384,512]{1,0:T(8,128)(2,1)} %copy-done.6) | copy-start | bytes 1179652
  216.8 54.4 %collective-permute-start.13 = (bf16[384,1024]{1,0:T(8,128)(2,1)}, bf16[384,1024]{1,0:T(8,128)(2,1)S(1)}, u32[]{:S(2)}, u32[]{:S(2)}) collective-permute-start(bf16[384,1024]{1,0:T(8,128)(2,1)} %get-tuple-element.86), channel_id=1, source_target_pairs={{0,2},{1,3},{2,0},{3,1},{4,6},{5,7},{6,4},{7,5},{8,10},{9,11},{10,... | collective-permute-start | bytes 2359304 | tf_op jit(solution)/shard_map/ppermute | solution.py:36
  218.4 53.4 %collective-permute-start.14 = (bf16[384,1024]{1,0:T(8,128)(2,1)}, bf16[384,1024]{1,0:T(8,128)(2,1)S(1)}, u32[]{:S(2)}, u32[]{:S(2)}) collective-permute-start(bf16[384,1024]{1,0:T(8,128)(2,1)} %get-tuple-element.87), channel_id=1, source_target_pairs={{0,3},{1,2},{2,1},{3,0},{4,7},{5,6},{6,5},{7,4},{8,11},{9,10},{10,... | collective-permute-start | bytes 2359304 | tf_op jit(solution)/shard_map/ppermute | solution.py:36
  218.9 69.2 %collective-permute-start.10 = (bf16[384,1024]{1,0:T(8,128)(2,1)S(1)}, bf16[384,1024]{1,0:T(8,128)(2,1)S(1)}, u32[]{:S(2)}, u32[]{:S(2)}) collective-permute-start(bf16[384,1024]{1,0:T(8,128)(2,1)S(1)} %get-tuple-element.83), channel_id=1, source_target_pairs={{0,2},{1,3},{2,0},{3,1},{4,6},{5,7},{6,4},{7,5},{8,10},{9,11},{10,... | collective-permute-start | bytes 2359304 | tf_op jit(solution)/shard_map/ppermute | solution.py:36
  234.3 62.9 %collective-permute-start.11 = (bf16[384,1024]{1,0:T(8,128)(2,1)S(1)}, bf16[384,1024]{1,0:T(8,128)(2,1)S(1)}, u32[]{:S(2)}, u32[]{:S(2)}) collective-permute-start(bf16[384,1024]{1,0:T(8,128)(2,1)S(1)} %get-tuple-element.84), channel_id=1, source_target_pairs={{0,3},{1,2},{2,1},{3,0},{4,7},{5,6},{6,5},{7,4},{8,11},{9,10},{10,... | collective-permute-start | bytes 2359304 | tf_op jit(solution)/shard_map/ppermute | solution.py:36
  236.7 60.4 %collective-permute-start.9 = (bf16[384,1024]{1,0:T(8,128)(2,1)S(1)}, bf16[384,1024]{1,0:T(8,128)(2,1)S(1)}, u32[]{:S(2)}, u32[]{:S(2)}) collective-permute-start(bf16[384,1024]{1,0:T(8,128)(2,1)S(1)} %get-tuple-element.82), channel_id=1, source_target_pairs={{0,1},{1,0},{2,3},{3,2},{4,5},{5,4},{6,7},{7,6},{8,9},{9,8},{10,11... | collective-permute-start | bytes 2359304 | tf_op jit(solution)/shard_map/ppermute | solution.py:36
  271.2 28.5 %collective-permute-start.5 = (bf16[384,512]{1,0:T(8,128)(2,1)S(1)}, bf16[384,512]{1,0:T(8,128)(2,1)S(1)}, u32[]{:S(2)}, u32[]{:S(2)}) collective-permute-start(bf16[384,512]{1,0:T(8,128)(2,1)S(1)} %get-tuple-element.72), channel_id=1, source_target_pairs={{0,1},{1,0},{2,3},{3,2},{4,5},{5,4},{6,7},{7,6},{8,9},{9,8},{10,11... | collective-permute-start | bytes 1179656 | tf_op jit(solution)/shard_map/ppermute | solution.py:36
  271.8 31.9 %collective-permute-start.6 = (bf16[384,512]{1,0:T(8,128)(2,1)S(1)}, bf16[384,512]{1,0:T(8,128)(2,1)S(1)}, u32[]{:S(2)}, u32[]{:S(2)}) collective-permute-start(bf16[384,512]{1,0:T(8,128)(2,1)S(1)} %get-tuple-element.73), channel_id=1, source_target_pairs={{0,2},{1,3},{2,0},{3,1},{4,6},{5,7},{6,4},{7,5},{8,10},{9,11},{10,... | collective-permute-start | bytes 1179656 | tf_op jit(solution)/shard_map/ppermute | solution.py:36
  288.1 15.6 %collective-permute-start.7 = (bf16[384,512]{1,0:T(8,128)(2,1)S(1)}, bf16[384,512]{1,0:T(8,128)(2,1)S(1)}, u32[]{:S(2)}, u32[]{:S(2)}) collective-permute-start(bf16[384,512]{1,0:T(8,128)(2,1)S(1)} %get-tuple-element.74), channel_id=1, source_target_pairs={{0,3},{1,2},{2,1},{3,0},{4,7},{5,6},{6,5},{7,4},{8,11},{9,10},{10,... | collective-permute-start | bytes 1179656 | tf_op jit(solution)/shard_map/ppermute | solution.py:36
  (9 other events, 132.0 us)

commit v3 on v2

--- a/solution.py
+++ b/solution.py
@@ -36,8 +36,71 @@
     return lax.ppermute(value, axis, [(source, source ^ flip) for source in range(count)])
 
 
+def pack_kernel(plan, rows, *rest):
+    count = len(plan)
+    keys, values = rest[:2]
+    outs = rest[2 : 2 + count]
+    scrs = rest[2 + count : 2 + 2 * count]
+    in_sems, out_sems = rest[2 + 2 * count :]
+    loads = []
+    for index, (layer, kv_first, kv_count) in enumerate(plan):
+        width = kv_count * HEAD_SIZE
+        for kind, array in enumerate((keys, values)):
+            loads.append(
+                pltpu.make_async_copy(
+                    array.at[layer, rows, pl.ds(kv_first * HEAD_SIZE, width)],
+                    scrs[index].at[:, pl.ds(kind * width, width)],
+                    in_sems.at[index, kind],
+                )
+            )
+    for load in loads:
+        load.start()
+    stores = []
+    for index in range(count):
+        loads[2 * index].wait()
+        loads[2 * index + 1].wait()
+        store = pltpu.make_async_copy(scrs[index], outs[index], out_sems.at[index])
+        store.start()
+        stores.append(store)
+    for store in stores:
+        store.wait()
+
+
+def pack_call(plan, keys, values):
+    tok_local = keys.shape[1]
+    any_spec = pl.BlockSpec(memory_space=pl.ANY)
+    sizes = [(WINDOW_LENGTH, 2 * kv_count * HEAD_SIZE) for _, _, kv_count in plan]
+    return pl.pallas_call(
+        functools.partial(pack_kernel, plan, pl.ds(tok_local - WINDOW_LENGTH, WINDOW_LENGTH)),
+        in_specs=[any_spec] * 2,
+        out_specs=[any_spec] * len(plan),
+        out_shape=[jax.ShapeDtypeStruct(size, jnp.bfloat16) for size in sizes],
+        scratch_shapes=[pltpu.VMEM(size, jnp.bfloat16) for size in sizes]
+        + [pltpu.SemaphoreType.DMA((len(plan), 2)), pltpu.SemaphoreType.DMA((len(plan),))],
+        compiler_params=pltpu.CompilerParams(vmem_limit_bytes=16 * 1024 * 1024),
+        cost_estimate=pl.CostEstimate(
+            flops=0, bytes_accessed=4 * sum(size[0] * size[1] for size in sizes), transcendentals=0
+        ),
+        name="pack",
+    )(keys, values)
+
+
 def band_kernel(
-    layer, kv_first, kv_count, owners, scal, q_ref, do_ref, out_ref, lse_ref, k_ref, v_ref, halo_ref, after, *rest
+    layer,
+    kv_first,
+    kv_count,
+    owners,
+    scal,
+    q_ref,
+    do_ref,
+    out_ref,
+    lse_ref,
+    k_ref,
+    v_ref,
+    k_halo,
+    v_halo,
+    after,
+    *rest,
 ):
     dq_bufs = rest[:owners]
     back_ref, part_ref, kx, vx, kt, acc, lse2_scr, delta_scr, dq_scr, sems = rest[owners:]
@@ -50,8 +113,8 @@
     win = scal[2 + layer]
     wide = group * TILE
 
-    kx[0:WINDOW_LENGTH] = halo_ref[:, 0:HEAD_SIZE]
-    vx[0:WINDOW_LENGTH] = halo_ref[:, HEAD_SIZE : 2 * HEAD_SIZE]
+    kx[0:WINDOW_LENGTH] = k_halo[...]
+    vx[0:WINDOW_LENGTH] = v_halo[...]
     kx[WINDOW_LENGTH:] = k_ref[0]
     vx[WINDOW_LENGTH:] = v_ref[0]
     kt[...] = kx[...].T
@@ -80,44 +143,70 @@
                 lse_ref[0, pl.ds(head + h, 1), start : start + TILE] * LOG2E
             )
 
-    def one_block(block, carry):
-        start = pl.multiple_of(block * TILE, TILE)
-        columns = pl.ds(pl.multiple_of(block * wide, wide), wide)
-        q2 = stacked(q_ref, start)
-        do2 = stacked(do_ref, start)
+    tiles = WINDOW_LENGTH // TILE + 1
+
+    def weights(start, tile, half, scores, grad_prob, lse2, delta):
+        place = tile - half
+        prob = jnp.exp2(scores * (SCALE * LOG2E) - lse2)
+        if place == tiles - 1:
+            seen = rows <= lanes
+        else:
+            bound = WINDOW_LENGTH - win - place * TILE
+            outside = jnp.logical_and(first_shard == 1, start + tile * TILE < WINDOW_LENGTH)
+            seen = rows > lanes + jnp.where(outside, FAR, bound)
+        prob = jnp.where(seen, prob, 0.0)
+        return prob.astype(jnp.bfloat16), (prob * (grad_prob - delta)).astype(jnp.bfloat16)
+
+    def one_pair(pair, carry):
+        start = pl.multiple_of(pair * 2 * TILE, 2 * TILE)
+        columns = pl.ds(pl.multiple_of(pair * 2 * wide, 2 * wide), 2 * wide)
+        q4 = jnp.concatenate([stacked(q_ref, start), stacked(q_ref, start + TILE)], 0)
+        do4 = jnp.concatenate([stacked(do_ref, start), stacked(do_ref, start + TILE)], 0)
         delta = delta_scr[0:1, columns]
         lse2 = lse2_scr[0:1, columns]
-        tiles = WINDOW_LENGTH // TILE + 1
-        span = pl.ds(start, tiles * TILE)
-        scores = dot(kx[span, :], q2, NT)
-        grad_prob = dot(vx[span, :], do2, NT)
-        prob_low = []
-        score_low = []
-        for tile in range(tiles):
-            part = slice(tile * TILE, (tile + 1) * TILE)
-            prob = jnp.exp2(scores[part] * (SCALE * LOG2E) - lse2)
-            if tile == tiles - 1:
-                seen = rows <= lanes
-            else:
-                bound = WINDOW_LENGTH - win - tile * TILE
-                outside = jnp.logical_and(first_shard == 1, start + tile * TILE < WINDOW_LENGTH)
-                seen = rows > lanes + jnp.where(outside, FAR, bound)
-            prob = jnp.where(seen, prob, 0.0)
-            prob_low.append(prob.astype(jnp.bfloat16))
-            score_low.append((prob * (grad_prob[part] - delta)).astype(jnp.bfloat16))
-        prob_low = jnp.concatenate(prob_low, 0)
-        score_low = jnp.concatenate(score_low, 0)
-        acc[span, HEAD_SIZE:] += dot(prob_low, do2)
-        acc[span, :HEAD_SIZE] += dot(score_low, q2)
-        dq_t = dot(kt[:, span], score_low)
-        dq = (dq_t.T * SCALE).astype(jnp.bfloat16)
-        for h in range(group):
-            dq_scr[step, pl.ds(start, TILE), h * HEAD_SIZE : (h + 1) * HEAD_SIZE] = dq[
-                h * TILE : (h + 1) * TILE
-            ]
+        score_lows = ([], [])
+
+        def finish(tile, halves, scores, grad_prob):
+            low = halves[0] * wide
+            high = (halves[-1] + 1) * wide
+            probs, grads = [], []
+            for half in halves:
+                mine = slice(half * wide - low, (half + 1) * wide - low)
+                ours = slice(half * wide, (half + 1) * wide)
+                prob_low, score_low = weights(
+                    start, tile, half, scores[:, mine], grad_prob[:, mine], lse2[:, ours], delta[:, ours]
+                )
+                probs.append(prob_low)
+                grads.append(score_low)
+                score_lows[half].append(score_low)
+            span = pl.ds(start + tile * TILE, TILE)
+            acc[span, HEAD_SIZE:] += dot(jnp.concatenate(probs, 1), do4[low:high])
+            acc[span, :HEAD_SIZE] += dot(jnp.concatenate(grads, 1), q4[low:high])
+
+        held = None
+        for tile in range(tiles + 1):
+            halves = [half for half in (0, 1) if 0 <= tile - half < tiles]
+            low = halves[0] * wide
+            high = (halves[-1] + 1) * wide
+            span = pl.ds(start + tile * TILE, TILE)
+            scores = dot(kx[span, :], q4[low:high], NT)
+            grad_prob = dot(vx[span, :], do4[low:high], NT)
+            if held is not None:
+                finish(*held)
+            held = (tile, halves, scores, grad_prob)
+        finish(*held)
+        for half in (0, 1):
+            begin = start + half * TILE
+            keys_t = kt[:, pl.ds(pl.multiple_of(begin, TILE), tiles * TILE)]
+            dq_t = dot(keys_t, jnp.concatenate(score_lows[half], 0))
+            dq = (dq_t.T * SCALE).astype(jnp.bfloat16)
+            for h in range(group):
+                dq_scr[step, pl.ds(begin, TILE), h * HEAD_SIZE : (h + 1) * HEAD_SIZE] = dq[
+                    h * TILE : (h + 1) * TILE
+                ]
         return carry
 
-    lax.fori_loop(0, tok_local // TILE, one_block, 0)
+    lax.fori_loop(0, tok_local // (2 * TILE), one_pair, 0)
 
     back_ref[:, :HEAD_SIZE] = (acc[0:WINDOW_LENGTH, :HEAD_SIZE] * SCALE).astype(jnp.bfloat16)
     back_ref[:, HEAD_SIZE:] = acc[0:WINDOW_LENGTH, HEAD_SIZE:].astype(jnp.bfloat16)
@@ -153,6 +242,7 @@
     group = queries.shape[2] // keys.shape[2]
     span = WINDOW_LENGTH + tok_local
     chunk = tok_local // owners
+    halo_kv = halo.shape[1] // (2 * HEAD_SIZE)
     q_spec = pl.BlockSpec((1, tok_local, group * HEAD_SIZE), lambda g: (layer, 0, kv_first + g))
     kv_spec = pl.BlockSpec((1, tok_local, HEAD_SIZE), lambda g: (layer, 0, kv_first + g))
     pairs = tok_local * (WINDOW_LENGTH + TILE) * group * kv_count
@@ -167,7 +257,8 @@
             pl.BlockSpec((1,) + log_norm.shape[1:], lambda g: (layer, 0, 0)),
             kv_spec,
             kv_spec,
-            pl.BlockSpec((WINDOW_LENGTH, 2 * HEAD_SIZE), lambda g: (0, column + g)),
+            pl.BlockSpec((WINDOW_LENGTH, HEAD_SIZE), lambda g: (0, column + g)),
+            pl.BlockSpec((WINDOW_LENGTH, HEAD_SIZE), lambda g: (0, halo_kv + column + g)),
             pl.BlockSpec(memory_space=pl.ANY),
         ],
         out_specs=[pl.BlockSpec(memory_space=pl.ANY)] * owners
@@ -193,19 +284,19 @@
             pltpu.VMEM((kv_count, tok_local, group * HEAD_SIZE), jnp.bfloat16),
             pltpu.SemaphoreType.DMA((kv_count, owners)),
         ],
-        compiler_params=pltpu.CompilerParams(vmem_limit_bytes=40 * 1024 * 1024),
+        compiler_params=pltpu.CompilerParams(vmem_limit_bytes=44 * 1024 * 1024),
         cost_estimate=pl.CostEstimate(
-            flops=pairs * 2 * HEAD_SIZE * 5 * 2,
+            flops=pairs * 2 * HEAD_SIZE * 5 * 4,
             bytes_accessed=8 * tok_local * group * kv_count * HEAD_SIZE,
             transcendentals=pairs,
         ),
         name="band",
-    )(scal, queries, grad_out, attn_out, log_norm, keys, values, halo, after)
+    )(scal, queries, grad_out, attn_out, log_norm, keys, values, halo, halo, after)
     return outs[:owners], outs[owners], outs[owners + 1]
 
 
-def finish_kernel(kv_count, owners, column, aliased, scal, part_ref, back_ref, *rest):
-    bufs = rest[owners if aliased else 0 :][:owners]
+def finish_kernel(kv_count, owners, column, skip, scal, part_ref, back_ref, *rest):
+    bufs = rest[skip:][:owners]
     scr, sems = rest[-2:]
     tok_local = part_ref.shape[0]
     chunk = tok_local // owners
@@ -245,21 +336,23 @@
                 copy.wait()
 
 
-def finish_call(kv_count, owners, column, scal, part, back, bufs):
+def finish_call(kv_count, owners, column, scal, part, back, bufs, after):
     tok_local = part.shape[0]
     chunk = tok_local // owners
     aliased = bufs is not None
     shape = jax.ShapeDtypeStruct((chunk, column + kv_count * 2 * HEAD_SIZE), jnp.bfloat16)
     any_spec = pl.BlockSpec(memory_space=pl.ANY)
     return pl.pallas_call(
-        functools.partial(finish_kernel, kv_count, owners, column, aliased),
+        functools.partial(
+            finish_kernel, kv_count, owners, column, len(after) + (owners if aliased else 0)
+        ),
         grid=(kv_count,),
         in_specs=[
             pl.BlockSpec(memory_space=pltpu.SMEM),
             pl.BlockSpec((tok_local, 2 * HEAD_SIZE), lambda g: (0, g)),
             pl.BlockSpec((WINDOW_LENGTH, 2 * HEAD_SIZE), lambda g: (0, g)),
         ]
-        + ([any_spec] * owners if aliased else []),
+        + [any_spec] * ((owners if aliased else 0) + len(after)),
         out_specs=[any_spec] * owners,
         out_shape=[shape] * owners,
         input_output_aliases={3 + i: i for i in range(owners)} if aliased else {},
@@ -272,7 +365,7 @@
             flops=0, bytes_accessed=16 * tok_local * kv_count * HEAD_SIZE, transcendentals=0
         ),
         name="finish",
-    )(scal, part, back, *(bufs if aliased else ()))
+    )(scal, part, back, *(bufs if aliased else ()), *after)
 
 
 def place_kernel(plan, owners, group, kv_local, aliased, scal, *rest):
@@ -350,36 +443,36 @@
             window.astype(jnp.int32),
         ]
     )
-    each = min(2, kv_local)
-    pieces = [
-        (layer, kv_first, each)
-        for layer in range(SLIDING_LAYERS)
-        for kv_first in range(0, kv_local, each)
-    ]
-
-    def halo_of(some):
-        parts = []
-        for layer, kv_first, kv_count in some:
-            for kv in range(kv_first, kv_first + kv_count):
-                columns = slice(kv * HEAD_SIZE, (kv + 1) * HEAD_SIZE)
-                parts.append(layer_keys_input[layer, tok_local - WINDOW_LENGTH :, columns])
-                parts.append(layer_values_input[layer, tok_local - WINDOW_LENGTH :, columns])
-        return shifted(jnp.concatenate(parts, 1), "ctx", 1)
-
-    first_halo = halo_of(pieces[:1])
-    other_halo = halo_of(pieces[1:])
-    halos = [(first_halo, 0)] + [(other_halo, index * each) for index in range(len(pieces) - 1)]
+    pieces = []
+    for layer in range(SLIDING_LAYERS):
+        kv_first = 0
+        while kv_first < kv_local:
+            kv_count = 1 if layer == 0 and kv_first < 2 else min(2, kv_local - kv_first)
+            pieces.append((layer, kv_first, kv_count))
+            kv_first += kv_count
+
+    plans = [[(0, 0, 1)], [(0, 1, kv_local - 1)], [(1, 0, kv_local)]]
+    packed = pack_call(plans[0], layer_keys_input, layer_values_input)
+    packed += pack_call(plans[1] + plans[2], layer_keys_input, layer_values_input)
+    halos = [shifted(block, "ctx", 1) for block in packed]
+
+    def halo_of(layer, kv_first):
+        if layer == 1:
+            return halos[2], kv_first
+        return (halos[0], 0) if kv_first == 0 else (halos[1], kv_first - 1)
 
     outs = None
     waiting = None
-
-    def send(plan, bufs, outs):
+    after = scal
+    sent = []
+
+    def send(plan, bufs):
         blocks = [bufs[0]] + [swapped(bufs[flip], "head", flip) for flip in range(1, owners)]
-        return place_call(plan, owners, group, kv_local, scal, blocks, outs)
-
-    after = scal
-    for piece, (halo, column) in zip(pieces, halos):
-        kv_count = piece[2]
+        sent.append((plan, blocks))
+
+    for index, piece in enumerate(pieces):
+        layer, kv_first, kv_count = piece
+        halo, column = halo_of(layer, kv_first)
         extra = 0 if waiting is None else 2 * waiting[0][2]
         bufs, back, part = band_call(
             piece,
@@ -401,16 +494,19 @@
         plan = [(0, piece)]
         if waiting is not None:
             old, old_part, old_back = waiting
+            before = sent[-1][1][1:]
             bufs = finish_call(
-                old[2], owners, kv_count * group * HEAD_SIZE, scal, old_part, old_back, bufs
+                old[2], owners, kv_count * group * HEAD_SIZE, scal, old_part, old_back, bufs, before
             )
             after = bufs[0]
             plan += [(1, old), (2, old)]
-        outs = send(plan, bufs, outs)
+        send(plan, bufs)
         waiting = (piece, part, back)
     old, old_part, old_back = waiting
-    bufs = finish_call(old[2], owners, 0, scal, old_part, old_back, None)
-    outs = send([(1, old), (2, old)], bufs, outs)
+    bufs = finish_call(old[2], owners, 0, scal, old_part, old_back, None, ())
+    send([(1, old), (2, old)], bufs)
+    for plan, blocks in sent:
+        outs = place_call(plan, owners, group, kv_local, scal, blocks, outs)
     return tuple(outs)
 
 

time: 307 us -> 233 us (0.76)
  waiting for transfers between devices: 109 us -> 39.3 us
  local copies, waits for them, and re-layouts: 23.8 us -> 5.73 us
  starting transfers between devices: 31 us -> 38.8 us
  Pallas kernels: 140 us -> 147 us
    ppermute x6 -> x8, waiting for transfers between devices: 44 us -> 4.47 us  [shifted(): lax.ppermute(value, axis, [(source, source + steps) for source in range(f...]
    ppermute x15 -> x18, waiting for transfers between devices: 65.2 us -> 34.9 us  [swapped(): lax.ppermute(value, axis, [(source, source ^ flip) for source in range(co...]
    unnamed x35 -> x32, local copies, waits for them, and re-layouts: 21 us -> 5.73 us
    ppermute x6 -> x8, starting transfers between devices: 12.2 us -> 16.5 us  [shifted(): lax.ppermute(value, axis, [(source, source + steps) for source in range(f...]
    ppermute x15 -> x18, starting transfers between devices: 18.9 us -> 22.3 us  [swapped(): lax.ppermute(value, axis, [(source, source ^ flip) for source in range(co...]
    pallas_call x0 -> x2, Pallas kernels: none -> 3.29 us  [pack_call(): pl.pallas_call(functools.partial(pack_kernel, plan, pl.ds(tok_local - WIN...]
    pallas_call x5 -> x6, Pallas kernels: 12.7 us -> 15.2 us  [place_call(): pl.pallas_call(functools.partial(place_kernel, plan, owners, group, kv_lo...]
    pallas_call x4 -> x5, Pallas kernels: 7.12 us -> 8.57 us  [finish_call(): pl.pallas_call(functools.partial(finish_kernel, kv_count, owners, column,...]
  transfers between devices with their start and end apart: 21 -> 26, of which waited for: 5 -> 8; matrix products, arithmetic and copies ran while one was open for 1% -> 0% of each run, Pallas kernels for 45% -> 62%
where the time goes in v3:
time: 233 us; the launch traced here: 232 us
  Pallas kernels  147 us (63%)
  waiting for transfers between devices  39.3 us (17%)
  starting transfers between devices  38.8 us (17%)
  local copies, waits for them, and re-layouts  5.73 us (2%)
    pallas_call x5, Pallas kernels, band_call(): pl.pallas_call(functools.partial(band_kernel, layer, kv_first, kv_count,...  120 us
    ppermute x18, waiting for transfers between devices, swapped(): lax.ppermute(value, axis, [(source, source ^ flip) for source in range(co...  34.9 us
    ppermute x18, starting transfers between devices, swapped(): lax.ppermute(value, axis, [(source, source ^ flip) for source in range(co...  22.3 us
    ppermute x8, starting transfers between devices, shifted(): lax.ppermute(value, axis, [(source, source + steps) for source in range(f...  16.5 us
    pallas_call x6, Pallas kernels, place_call(): pl.pallas_call(functools.partial(place_kernel, plan, owners, group, kv_lo...  15.2 us
    pallas_call x5, Pallas kernels, finish_call(): pl.pallas_call(functools.partial(finish_kernel, kv_count, owners, column,...  8.57 us
    unnamed x32, local copies, waits for them, and re-layouts  5.73 us
  transfers between devices with their start and end apart: 26, of which 8 were waited for; matrix products, arithmetic and copies ran while one was open for 0% of the time, Pallas kernels for 62%

profile of v3, /device:TPU:24, one launch (start us, length us, event | category | flops | bytes accessed | tf_op | source)
XLA Modules:
  0.0 232.2 jit_solution(18069976447897569993)
XLA Ops:
  5.4 2.2 collective-permute-start.2
  7.6 2.4 %pack.2 = (bf16[1024,768]{1,0:T(8,128)(2,1)}, bf16[1024,1024]{1,0:T(8,128)(2,1)}) custom-call(bf16[2,1536,512]{2,1,0:T(8,128)(2,1)S(1)} %copy-done, bf16[2,1536,512]{2,1,0:T(8,128)(2,1)S(1)} %copy-done.2), custom_call_target="tpu_custom_call" | custom-call | bytes 7340032 | tf_op jit(solution)/shard_map/pack/pallas_call | solution.py:73
  9.9 1.9 collective-permute-start.1
  13.9 2.5 %collective-permute-done.2.k_halo.v_halo = bf16[1024,256]{1,0:T(8,128)(2,1)} collective-permute-done((bf16[1024,256]{1,0:T(8,128)(2,1)}, bf16[1024,256]{1,0:T(8,128)(2,1)}, u32[]{:S(2)}, u32[]{:S(2)}) %collective-permute-start.2) | collective-permute-done | bytes 524320 | tf_op jit(solution)/shard_map/ppermute | solution.py:31
  18.3 15.9 %band.5 = (bf16[384,256]{1,0:T(8,128)(2,1)S(1)}, bf16[384,256]{1,0:T(8,128)(2,1)S(1)}, bf16[384,256]{1,0:T(8,128)(2,1)S(1)}, bf16[384,256]{1,0:T(8,128)(2,1)S(1)...) custom-call(s32[4]{0:T(128)S(1)} %pad_add_fusion.scal.after, bf16[2,1536,1024]{2,1,0:T(8,128)(2,1)} %q_ref.9, ...), custom_call_target="tpu_custom_call" | custom-call | flops 20132659200 | bytes 3145728 | tf_op jit(solution)/shard_map/band/pallas_call | solution.py:249
  39.8 15.1 %band.6 = (bf16[384,512]{1,0:T(8,128)(2,1)S(1)}, bf16[384,512]{1,0:T(8,128)(2,1)S(1)}, bf16[384,512]{1,0:T(8,128)(2,1)S(1)}, bf16[384,512]{1,0:T(8,128)(2,1)S(1)...) custom-call(s32[4]{0:T(128)S(1)} %pad_add_fusion.scal.after, bf16[2,1536,1024]{2,1,0:T(8,128)(2,1)} %q_ref.9, ...), custom_call_target="tpu_custom_call" | custom-call | flops 20132659200 | bytes 3145728 | tf_op jit(solution)/shard_map/band/pallas_call | solution.py:249
  61.5 30.0 %band.7 = (bf16[384,768]{1,0:T(8,128)(2,1)S(1)}, bf16[384,768]{1,0:T(8,128)(2,1)S(1)}, bf16[384,768]{1,0:T(8,128)(2,1)S(1)}, bf16[384,768]{1,0:T(8,128)(2,1)}, b...) custom-call(s32[4]{0:T(128)S(1)} %pad_add_fusion.scal.after, bf16[2,1536,1024]{2,1,0:T(8,128)(2,1)} %q_ref.9, ...), custom_call_target="tpu_custom_call" | custom-call | flops 40265318400 | bytes 6291456 | tf_op jit(solution)/shard_map/band/pallas_call | solution.py:249
  91.5 2.6 %collective-permute-start.7 = (bf16[1024,512]{1,0:T(8,128)(2,1)}, bf16[1024,512]{1,0:T(8,128)(2,1)}, u32[]{:S(2)}, u32[]{:S(2)}) collective-permute-start(bf16[1024,512]{1,0:T(8,128)(2,1)} %get-tuple-element.83), channel_id=1, source_target_pairs={{4,0},{8,4},{12,8},{16,12},{20,16},{24,20},{28,24},{5,1},{9,5},{13... | collective-permute-start | bytes 3145736 | tf_op jit(solution)/shard_map/ppermute | solution.py:31
  99.4 30.0 %band.8 = (bf16[384,1024]{1,0:T(8,128)(2,1)S(1)}, bf16[384,1024]{1,0:T(8,128)(2,1)}, bf16[384,1024]{1,0:T(8,128)(2,1)}, bf16[384,1024]{1,0:T(8,128)(2,1)}, bf16[...) custom-call(s32[4]{0:T(128)S(1)} %pad_add_fusion.scal.after, bf16[2,1536,1024]{2,1,0:T(8,128)(2,1)} %q_ref.9, ...), custom_call_target="tpu_custom_call" | custom-call | flops 40265318400 | bytes 6291456 | tf_op jit(solution)/shard_map/band/pallas_call | solution.py:249
  129.4 2.1 collective-permute-start.19
  131.6 2.5 %finish.7 = (bf16[384,1024]{1,0:T(8,128)(2,1)S(1)}, bf16[384,1024]{1,0:T(8,128)(2,1)}, bf16[384,1024]{1,0:T(8,128)(2,1)}, bf16[384,1024]{1,0:T(8,128)(2,1)}) custom-call(s32[4]{0:T(128)S(1)} %pad_add_fusion.scal.after, f32[1536,512]{1,0:T(8,128)S(1)} %get-tuple-element.82.part_ref, ...), custom_call_target="tpu_custom_call", output_to_operand_aliasing={{0}: (3, {}), {1}: (4, {}), {2}: (5, {}), {3}: (6, {})} | custom-call | bytes 6291456 | tf_op jit(solution)/shard_map/finish/pallas_call | solution.py:345
  137.7 28.8 %band.9 = (bf16[384,1024]{1,0:T(8,128)(2,1)S(1)}, bf16[384,1024]{1,0:T(8,128)(2,1)S(1)}, bf16[384,1024]{1,0:T(8,128)(2,1)S(1)}, bf16[384,1024]{1,0:T(8,128)(2,1)...) custom-call(s32[4]{0:T(128)S(1)} %pad_add_fusion.scal.after, bf16[2,1536,1024]{2,1,0:T(8,128)(2,1)} %q_ref.9, ...), custom_call_target="tpu_custom_call" | custom-call | flops 40265318400 | bytes 6291456 | tf_op jit(solution)/shard_map/band/pallas_call | solution.py:249
  168.4 4.7 %collective-permute-done.21.rest_5_.rest_2_ = bf16[384,1024]{1,0:T(8,128)(2,1)S(1)} collective-permute-done((bf16[384,1024]{1,0:T(8,128)(2,1)}, bf16[384,1024]{1,0:T(8,128)(2,1)S(1)}, u32[]{:S(2)}, u32[]{:S(2)}) %collective-permute-start.21) | collective-permute-done | bytes 786464 | tf_op jit(solution)/shard_map/ppermute | solution.py:36
  173.1 2.0 finish.9
  185.2 10.5 %collective-permute-done.23.rest_1_ = bf16[384,1024]{1,0:T(8,128)(2,1)S(1)} collective-permute-done((bf16[384,1024]{1,0:T(8,128)(2,1)S(1)}, bf16[384,1024]{1,0:T(8,128)(2,1)S(1)}, u32[]{:S(2)}, u32[]{:S(2)}) %collective-permute-start.23) | collective-permute-done | bytes 786464 | tf_op jit(solution)/shard_map/ppermute | solution.py:36
  197.2 2.5 %place.6 = (bf16[2,384,4096]{2,1,0:T(8,128)(2,1)}, bf16[2,384,2048]{2,1,0:T(8,128)(2,1)}, bf16[2,384,2048]{2,1,0:T(8,128)(2,1)}) custom-call(s32[4]{0:T(128)S(1)} %pad_add_fusion.scal.after, bf16[384,256]{1,0:T(8,128)(2,1)S(1)} %copy-done.11, bf16[384,256]{1,0:T(8,128)(2,1)S(1)} %copy-done.5, bf16[384,256]{1,0:T(8,128)(2,1)S(1)} %copy-done.7, ...), custom_call_target="tpu_custom_call" | custom-call | bytes 1572864 | tf_op jit(solution)/shard_map/place/pallas_call | solution.py:414
  199.7 2.6 %place.7 = (bf16[2,384,4096]{2,1,0:T(8,128)(2,1)}, bf16[2,384,2048]{2,1,0:T(8,128)(2,1)}, bf16[2,384,2048]{2,1,0:T(8,128)(2,1)}) custom-call(s32[4]{0:T(128)S(1)} %pad_add_fusion.scal.after, bf16[384,512]{1,0:T(8,128)(2,1)S(1)} %get-tuple-element.81.after.rest_0_, ...), custom_call_target="tpu_custom_call", output_to_operand_aliasing={{0}: (5, {}), {1}: (6, {}), {2}: (7, {})} | custom-call | bytes 3145728 | tf_op jit(solution)/shard_map/place/pallas_call | solution.py:414
  202.2 2.6 %place.8 = (bf16[2,384,4096]{2,1,0:T(8,128)(2,1)}, bf16[2,384,2048]{2,1,0:T(8,128)(2,1)}, bf16[2,384,2048]{2,1,0:T(8,128)(2,1)}) custom-call(s32[4]{0:T(128)S(1)} %pad_add_fusion.scal.after, bf16[384,768]{1,0:T(8,128)(2,1)S(1)} %get-tuple-element.93.after.rest_0_, ...), custom_call_target="tpu_custom_call", output_to_operand_aliasing={{0}: (5, {}), {1}: (6, {}), {2}: (7, {})} | custom-call | bytes 4718592 | tf_op jit(solution)/shard_map/place/pallas_call | solution.py:414
  204.8 2.5 %place.9 = (bf16[2,384,4096]{2,1,0:T(8,128)(2,1)}, bf16[2,384,2048]{2,1,0:T(8,128)(2,1)}, bf16[2,384,2048]{2,1,0:T(8,128)(2,1)}) custom-call(s32[4]{0:T(128)S(1)} %pad_add_fusion.scal.after, bf16[384,1024]{1,0:T(8,128)(2,1)S(1)} %get-tuple-element.101.after.rest_0_, ...), custom_call_target="tpu_custom_call", output_to_operand_aliasing={{0}: (5, {}), {1}: (6, {}), {2}: (7, {})} | custom-call | bytes 6291456 | tf_op jit(solution)/shard_map/place/pallas_call | solution.py:414
  207.4 5.6 %collective-permute-done.24.rest_2_ = bf16[384,1024]{1,0:T(8,128)(2,1)S(1)} collective-permute-done((bf16[384,1024]{1,0:T(8,128)(2,1)S(1)}, bf16[384,1024]{1,0:T(8,128)(2,1)S(1)}, u32[]{:S(2)}, u32[]{:S(2)}) %collective-permute-start.24) | collective-permute-done | bytes 786464 | tf_op jit(solution)/shard_map/ppermute | solution.py:36
  213.5 2.5 %place.10 = (bf16[2,384,4096]{2,1,0:T(8,128)(2,1)}, bf16[2,384,2048]{2,1,0:T(8,128)(2,1)}, bf16[2,384,2048]{2,1,0:T(8,128)(2,1)}) custom-call(s32[4]{0:T(128)S(1)} %pad_add_fusion.scal.after, bf16[384,1024]{1,0:T(8,128)(2,1)S(1)} %get-tuple-element.117.rest_0_, ...), custom_call_target="tpu_custom_call", output_to_operand_aliasing={{0}: (5, {}), {1}: (6, {}), {2}: (7, {})} | custom-call | bytes 6291456 | tf_op jit(solution)/shard_map/place/pallas_call | solution.py:414
  216.1 4.9 %collective-permute-done.16.rest_1_ = bf16[384,512]{1,0:T(8,128)(2,1)S(1)} collective-permute-done((bf16[384,512]{1,0:T(8,128)(2,1)S(1)}, bf16[384,512]{1,0:T(8,128)(2,1)S(1)}, u32[]{:S(2)}, u32[]{:S(2)}) %collective-permute-start.16) | collective-permute-done | bytes 393248 | tf_op jit(solution)/shard_map/ppermute | solution.py:36
  221.0 8.5 %collective-permute-done.18.rest_3_ = bf16[384,512]{1,0:T(8,128)(2,1)S(1)} collective-permute-done((bf16[384,512]{1,0:T(8,128)(2,1)S(1)}, bf16[384,512]{1,0:T(8,128)(2,1)S(1)}, u32[]{:S(2)}, u32[]{:S(2)}) %collective-permute-start.18) | collective-permute-done | bytes 393248 | tf_op jit(solution)/shard_map/ppermute | solution.py:36
  229.5 2.5 %place.11 = (bf16[2,384,4096]{2,1,0:T(8,128)(2,1)}, bf16[2,384,2048]{2,1,0:T(8,128)(2,1)}, bf16[2,384,2048]{2,1,0:T(8,128)(2,1)}) custom-call(s32[4]{0:T(128)S(1)} %pad_add_fusion.scal.after, bf16[384,512]{1,0:T(8,128)(2,1)S(1)} %get-tuple-element.104.rest_0_, ...), custom_call_target="tpu_custom_call", output_to_operand_aliasing={{0}: (5, {}), {1}: (6, {}), {2}: (7, {})} | custom-call | bytes 3145728 | tf_op jit(solution)/shard_map/place/pallas_call | solution.py:414
  (79 shorter events, 43.2 us)
Async XLA Ops:
  9.9 27.9 %collective-permute-start.1 = (bf16[1024,768]{1,0:T(8,128)(2,1)}, bf16[1024,768]{1,0:T(8,128)(2,1)}, u32[]{:S(2)}, u32[]{:S(2)}) collective-permute-start(bf16[1024,768]{1,0:T(8,128)(2,1)} %get-tuple-element.71), channel_id=1, source_target_pairs={{0,4},{4,8},{8,12},{12,16},{16,20},{20,24},{24,28},{1,5},{5,9},{9,... | collective-permute-start | bytes 4718600 | tf_op jit(solution)/shard_map/ppermute | solution.py:31
  11.9 87.5 %collective-permute-start = (bf16[1024,1024]{1,0:T(8,128)(2,1)}, bf16[1024,1024]{1,0:T(8,128)(2,1)}, u32[]{:S(2)}, u32[]{:S(2)}) collective-permute-start(bf16[1024,1024]{1,0:T(8,128)(2,1)} %get-tuple-element.70), channel_id=1, source_target_pairs={{0,4},{4,8},{8,12},{12,16},{16,20},{20,24},{24,28},{1,5},{5,9},{9,... | collective-permute-start | bytes 6291464 | tf_op jit(solution)/shard_map/ppermute | solution.py:31
  34.3 20.6 %collective-permute-start.4 = (bf16[384,256]{1,0:T(8,128)(2,1)S(1)}, bf16[384,256]{1,0:T(8,128)(2,1)S(1)}, u32[]{:S(2)}, u32[]{:S(2)}) collective-permute-start(bf16[384,256]{1,0:T(8,128)(2,1)S(1)} %get-tuple-element.78), channel_id=1, source_target_pairs={{0,1},{1,0},{2,3},{3,2},{4,5},{5,4},{6,7},{7,6},{8,9},{9,8},{10,11... | collective-permute-start | bytes 589832 | tf_op jit(solution)/shard_map/ppermute | solution.py:36
  35.9 19.1 %collective-permute-start.5 = (bf16[384,256]{1,0:T(8,128)(2,1)S(1)}, bf16[384,256]{1,0:T(8,128)(2,1)S(1)}, u32[]{:S(2)}, u32[]{:S(2)}) collective-permute-start(bf16[384,256]{1,0:T(8,128)(2,1)S(1)} %get-tuple-element.79), channel_id=1, source_target_pairs={{0,2},{1,3},{2,0},{3,1},{4,6},{5,7},{6,4},{7,5},{8,10},{9,11},{10,... | collective-permute-start | bytes 589832 | tf_op jit(solution)/shard_map/ppermute | solution.py:36
  37.4 17.6 %collective-permute-start.6 = (bf16[384,256]{1,0:T(8,128)(2,1)S(1)}, bf16[384,256]{1,0:T(8,128)(2,1)S(1)}, u32[]{:S(2)}, u32[]{:S(2)}) collective-permute-start(bf16[384,256]{1,0:T(8,128)(2,1)S(1)} %get-tuple-element.80), channel_id=1, source_target_pairs={{0,3},{1,2},{2,1},{3,0},{4,7},{5,6},{6,5},{7,4},{8,11},{9,10},{10,... | collective-permute-start | bytes 589832 | tf_op jit(solution)/shard_map/ppermute | solution.py:36
  37.9 17.1 %collective-permute-start.3 = (bf16[1024,256]{1,0:T(8,128)(2,1)S(1)}, bf16[1024,256]{1,0:T(8,128)(2,1)S(1)}, u32[]{:S(2)}, u32[]{:S(2)}) collective-permute-start(bf16[1024,256]{1,0:T(8,128)(2,1)S(1)} %get-tuple-element.73), channel_id=1, source_target_pairs={{4,0},{8,4},{12,8},{16,12},{20,16},{24,20},{28,24},{5,1},{9,5},{13... | collective-permute-start | bytes 1572872 | tf_op jit(solution)/shard_map/ppermute | solution.py:31
  56.0 35.5 %collective-permute-start.10 = (bf16[384,512]{1,0:T(8,128)(2,1)S(1)}, bf16[384,512]{1,0:T(8,128)(2,1)S(1)}, u32[]{:S(2)}, u32[]{:S(2)}) collective-permute-start(bf16[384,512]{1,0:T(8,128)(2,1)S(1)} %get-tuple-element.91), channel_id=1, source_target_pairs={{0,2},{1,3},{2,0},{3,1},{4,6},{5,7},{6,4},{7,5},{8,10},{9,11},{10,... | collective-permute-start | bytes 1179656 | tf_op jit(solution)/shard_map/ppermute | solution.py:36
  57.6 36.6 %collective-permute-start.11 = (bf16[384,512]{1,0:T(8,128)(2,1)S(1)}, bf16[384,512]{1,0:T(8,128)(2,1)S(1)}, u32[]{:S(2)}, u32[]{:S(2)}) collective-permute-start(bf16[384,512]{1,0:T(8,128)(2,1)S(1)} %get-tuple-element.92), channel_id=1, source_target_pairs={{0,3},{1,2},{2,1},{3,0},{4,7},{5,6},{6,5},{7,4},{8,11},{9,10},{10,... | collective-permute-start | bytes 1179656 | tf_op jit(solution)/shard_map/ppermute | solution.py:36
  59.0 35.2 %collective-permute-start.9 = (bf16[384,512]{1,0:T(8,128)(2,1)S(1)}, bf16[384,512]{1,0:T(8,128)(2,1)S(1)}, u32[]{:S(2)}, u32[]{:S(2)}) collective-permute-start(bf16[384,512]{1,0:T(8,128)(2,1)S(1)} %get-tuple-element.90), channel_id=1, source_target_pairs={{0,1},{1,0},{2,3},{3,2},{4,5},{5,4},{6,7},{7,6},{8,9},{9,8},{10,11... | collective-permute-start | bytes 1179656 | tf_op jit(solution)/shard_map/ppermute | solution.py:36
  59.5 34.6 %collective-permute-start.8 = (bf16[1024,256]{1,0:T(8,128)(2,1)S(1)}, bf16[1024,256]{1,0:T(8,128)(2,1)S(1)}, u32[]{:S(2)}, u32[]{:S(2)}) collective-permute-start(bf16[1024,256]{1,0:T(8,128)(2,1)S(1)} %get-tuple-element.85), channel_id=1, source_target_pairs={{4,0},{8,4},{12,8},{16,12},{20,16},{24,20},{28,24},{5,1},{9,5},{13... | collective-permute-start | bytes 1572872 | tf_op jit(solution)/shard_map/ppermute | solution.py:31
  91.5 40.0 %collective-permute-start.7 = (bf16[1024,512]{1,0:T(8,128)(2,1)}, bf16[1024,512]{1,0:T(8,128)(2,1)}, u32[]{:S(2)}, u32[]{:S(2)}) collective-permute-start(bf16[1024,512]{1,0:T(8,128)(2,1)} %get-tuple-element.83), channel_id=1, source_target_pairs={{4,0},{8,4},{12,8},{16,12},{20,16},{24,20},{28,24},{5,1},{9,5},{13... | collective-permute-start | bytes 3145736 | tf_op jit(solution)/shard_map/ppermute | solution.py:31
  95.8 35.7 %collective-permute-start.12 = (bf16[384,768]{1,0:T(8,128)(2,1)S(1)}, bf16[384,768]{1,0:T(8,128)(2,1)S(1)}, u32[]{:S(2)}, u32[]{:S(2)}) collective-permute-start(bf16[384,768]{1,0:T(8,128)(2,1)S(1)} %get-tuple-element.98), channel_id=1, source_target_pairs={{0,1},{1,0},{2,3},{3,2},{4,5},{5,4},{6,7},{7,6},{8,9},{9,8},{10,11... | collective-permute-start | bytes 1769480 | tf_op jit(solution)/shard_map/ppermute | solution.py:36
  97.4 34.2 %collective-permute-start.13 = (bf16[384,768]{1,0:T(8,128)(2,1)S(1)}, bf16[384,768]{1,0:T(8,128)(2,1)S(1)}, u32[]{:S(2)}, u32[]{:S(2)}) collective-permute-start(bf16[384,768]{1,0:T(8,128)(2,1)S(1)} %get-tuple-element.99), channel_id=1, source_target_pairs={{0,2},{1,3},{2,0},{3,1},{4,6},{5,7},{6,4},{7,5},{8,10},{9,11},{10,... | collective-permute-start | bytes 1769480 | tf_op jit(solution)/shard_map/ppermute | solution.py:36
  98.9 32.7 %collective-permute-start.14 = (bf16[384,768]{1,0:T(8,128)(2,1)}, bf16[384,768]{1,0:T(8,128)(2,1)S(1)}, u32[]{:S(2)}, u32[]{:S(2)}) collective-permute-start(bf16[384,768]{1,0:T(8,128)(2,1)} %get-tuple-element.100), channel_id=1, source_target_pairs={{0,3},{1,2},{2,1},{3,0},{4,7},{5,6},{6,5},{7,4},{8,11},{9,10},{10,... | collective-permute-start | bytes 1769480 | tf_op jit(solution)/shard_map/ppermute | solution.py:36
  129.4 39.0 %collective-permute-start.19 = (bf16[1024,512]{1,0:T(8,128)(2,1)}, bf16[1024,512]{1,0:T(8,128)(2,1)}, u32[]{:S(2)}, u32[]{:S(2)}) collective-permute-start(bf16[1024,512]{1,0:T(8,128)(2,1)} %get-tuple-element.109), channel_id=1, source_target_pairs={{4,0},{8,4},{12,8},{16,12},{20,16},{24,20},{28,24},{5,1},{9,5},{13... | collective-permute-start | bytes 3145736 | tf_op jit(solution)/shard_map/ppermute | solution.py:31
  134.1 34.3 %collective-permute-start.20 = (bf16[384,1024]{1,0:T(8,128)(2,1)}, bf16[384,1024]{1,0:T(8,128)(2,1)S(1)}, u32[]{:S(2)}, u32[]{:S(2)}) collective-permute-start(bf16[384,1024]{1,0:T(8,128)(2,1)} %get-tuple-element.114), channel_id=1, source_target_pairs={{0,1},{1,0},{2,3},{3,2},{4,5},{5,4},{6,7},{7,6},{8,9},{9,8},{10,11... | collective-permute-start | bytes 2359304 | tf_op jit(solution)/shard_map/ppermute | solution.py:36
  135.7 37.5 %collective-permute-start.21 = (bf16[384,1024]{1,0:T(8,128)(2,1)}, bf16[384,1024]{1,0:T(8,128)(2,1)S(1)}, u32[]{:S(2)}, u32[]{:S(2)}) collective-permute-start(bf16[384,1024]{1,0:T(8,128)(2,1)} %get-tuple-element.115), channel_id=1, source_target_pairs={{0,2},{1,3},{2,0},{3,1},{4,6},{5,7},{6,4},{7,5},{8,10},{9,11},{10,... | collective-permute-start | bytes 2359304 | tf_op jit(solution)/shard_map/ppermute | solution.py:36
  137.2 36.0 %collective-permute-start.22 = (bf16[384,1024]{1,0:T(8,128)(2,1)}, bf16[384,1024]{1,0:T(8,128)(2,1)S(1)}, u32[]{:S(2)}, u32[]{:S(2)}) collective-permute-start(bf16[384,1024]{1,0:T(8,128)(2,1)} %get-tuple-element.116), channel_id=1, source_target_pairs={{0,3},{1,2},{2,1},{3,0},{4,7},{5,6},{6,5},{7,4},{8,11},{9,10},{10,... | collective-permute-start | bytes 2359304 | tf_op jit(solution)/shard_map/ppermute | solution.py:36
  175.2 20.5 %collective-permute-start.23 = (bf16[384,1024]{1,0:T(8,128)(2,1)S(1)}, bf16[384,1024]{1,0:T(8,128)(2,1)S(1)}, u32[]{:S(2)}, u32[]{:S(2)}) collective-permute-start(bf16[384,1024]{1,0:T(8,128)(2,1)S(1)} %get-tuple-element.118), channel_id=1, source_target_pairs={{0,1},{1,0},{2,3},{3,2},{4,5},{5,4},{6,7},{7,6},{8,9},{9,8},{10,11... | collective-permute-start | bytes 2359304 | tf_op jit(solution)/shard_map/ppermute | solution.py:36
  176.0 37.0 %collective-permute-start.24 = (bf16[384,1024]{1,0:T(8,128)(2,1)S(1)}, bf16[384,1024]{1,0:T(8,128)(2,1)S(1)}, u32[]{:S(2)}, u32[]{:S(2)}) collective-permute-start(bf16[384,1024]{1,0:T(8,128)(2,1)S(1)} %get-tuple-element.119), channel_id=1, source_target_pairs={{0,2},{1,3},{2,0},{3,1},{4,6},{5,7},{6,4},{7,5},{8,10},{9,11},{10,... | collective-permute-start | bytes 2359304 | tf_op jit(solution)/shard_map/ppermute | solution.py:36
  177.3 36.2 %collective-permute-start.25 = (bf16[384,1024]{1,0:T(8,128)(2,1)S(1)}, bf16[384,1024]{1,0:T(8,128)(2,1)S(1)}, u32[]{:S(2)}, u32[]{:S(2)}) collective-permute-start(bf16[384,1024]{1,0:T(8,128)(2,1)S(1)} %get-tuple-element.120), channel_id=1, source_target_pairs={{0,3},{1,2},{2,1},{3,0},{4,7},{5,6},{6,5},{7,4},{8,11},{9,10},{10,... | collective-permute-start | bytes 2359304 | tf_op jit(solution)/shard_map/ppermute | solution.py:36
  182.1 38.9 %collective-permute-start.16 = (bf16[384,512]{1,0:T(8,128)(2,1)S(1)}, bf16[384,512]{1,0:T(8,128)(2,1)S(1)}, u32[]{:S(2)}, u32[]{:S(2)}) collective-permute-start(bf16[384,512]{1,0:T(8,128)(2,1)S(1)} %get-tuple-element.105), channel_id=1, source_target_pairs={{0,1},{1,0},{2,3},{3,2},{4,5},{5,4},{6,7},{7,6},{8,9},{9,8},{10,11... | collective-permute-start | bytes 1179656 | tf_op jit(solution)/shard_map/ppermute | solution.py:36
  183.6 37.4 %collective-permute-start.17 = (bf16[384,512]{1,0:T(8,128)(2,1)S(1)}, bf16[384,512]{1,0:T(8,128)(2,1)S(1)}, u32[]{:S(2)}, u32[]{:S(2)}) collective-permute-start(bf16[384,512]{1,0:T(8,128)(2,1)S(1)} %get-tuple-element.106), channel_id=1, source_target_pairs={{0,2},{1,3},{2,0},{3,1},{4,6},{5,7},{6,4},{7,5},{8,10},{9,11},{10,... | collective-permute-start | bytes 1179656 | tf_op jit(solution)/shard_map/ppermute | solution.py:36
  195.7 33.9 %collective-permute-start.18 = (bf16[384,512]{1,0:T(8,128)(2,1)S(1)}, bf16[384,512]{1,0:T(8,128)(2,1)S(1)}, u32[]{:S(2)}, u32[]{:S(2)}) collective-permute-start(bf16[384,512]{1,0:T(8,128)(2,1)S(1)} %get-tuple-element.107), channel_id=1, source_target_pairs={{0,3},{1,2},{2,1},{3,0},{4,7},{5,6},{6,5},{7,4},{8,11},{9,10},{10,... | collective-permute-start | bytes 1179656 | tf_op jit(solution)/shard_map/ppermute | solution.py:36
  (18 other events, 279.1 us)
